TPU v7x, 768 devices: a whole 4x8x12 slice. The times are simulated.
768 devices in a mesh: grid: 96 (over y, z), mem: 8 (over x, core).
Axes of the slice: x: 4, y: 8, z: 12, core: 2. Of those that a mesh axis runs over, the one named last changes fastest.
Arguments:
- background_elapsed_years: float32 [128, 4, 96, 1440], P('mem', None, 'grid'), may hold values from -6 to 6
- currents: float32 [2, 4, 96, 1440], P(None, None, 'grid'), may hold values from -0.1 to 0.1
- diffusivity: float32 [4, 96, 1440], P(None, 'grid'), may hold values from 0.01 to 0.1
- sea_mask: int32 [96, 1440], P('grid'), may hold values 0 or 1
- observed_cell: int32 [49152], P('grid'), may hold values from 0 to 1439
- measured_layer_number: int32 [49152], P('grid'), may hold values from 0 to 3
- live_counts: int32 [96], P('grid'), may hold values from 170 to 512, as said below
- observed_value: float32 [49152], P('grid'), may hold values from -5 to 5
- error_variance: float32 [49152], P('grid'), may hold values from 2 to 32
Outputs:
- analysis: float32 [128, 4, 96, 1440], P('mem', None, 'grid')
Inputs may be any that keep to these rules, and one draw needn't show every extreme that they name: `live_counts`: slots of a block at or past its count are not observations; some block has all 512 slots live and some block exactly 170. `observed_cell`: a cell is its latitude row within the block times 1440 plus its longitude.
All inputs are finite; a program needn't handle non-finite values. No bound on the sum of `sea_mask` on one device may be relied on, other than what follows from the above.
Results may differ from a plain program's by a relative error of at most 0.000071.
Values sent between devices are 32-bit elements; how exact they have to be, the bound alone decides.
A program may use at most 32 MiB of HBM per device.

v0:
```python
import math

import jax
import jax.numpy as jnp
from jax import lax
from jax.sharding import PartitionSpec as P

STEPS = 4


VERTICAL_MIX = 0.05
AGE_RATE = 0.25
SURFACE_RELAX = 0.5
HIGHEST = lax.Precision.HIGHEST


def padded_2(x, sides, width):
    for axis, dim in sides:
        count, length = (lax.axis_size(axis), x.shape[dim])
        up = [(i, (i + 1) % count) for i in range(count - 1)]
        down = [(j, i) for i, j in up]
        last = lax.slice_in_dim(x, length - width, length, axis=dim)
        leading = lax.slice_in_dim(x, 0, width, axis=dim)
        before = lax.ppermute(last, axis, up)
        after = lax.ppermute(leading, axis, down)
        x = jnp.concatenate([before, x, after], axis=dim)
    return x


def advance(state, padded, zonal_speed, kappa, north_speed, padded_kappa, sea_float, padded_sea):
    east_speed = 0.5 * (zonal_speed + jnp.roll(zonal_speed, -1, -1))
    east_kappa = 0.5 * (kappa + jnp.roll(kappa, -1, -1))
    east_open = sea_float * jnp.roll(sea_float, -1, -1)
    east_value = jnp.roll(state, -1, -1)
    zonal_flux = east_open * (
        jnp.maximum(east_speed, 0.0) * state
        + jnp.minimum(east_speed, 0.0) * east_value
        - east_kappa * (east_value - state)
    )
    face_speed = 0.5 * (north_speed[..., :-1, :] + north_speed[..., 1:, :])
    face_kappa = 0.5 * (padded_kappa[..., :-1, :] + padded_kappa[..., 1:, :])
    face_open = padded_sea[:-1] * padded_sea[1:]
    below_rows = padded[..., :-1, :]
    above_rows = padded[..., 1:, :]
    north_flux = face_open * (
        jnp.maximum(face_speed, 0.0) * below_rows
        + jnp.minimum(face_speed, 0.0) * above_rows
        - face_kappa * (above_rows - below_rows)
    )
    change = -(zonal_flux - jnp.roll(zonal_flux, 1, -1)) - (
        north_flux[..., 1:, :] - north_flux[..., :-1, :]
    )
    vertical = VERTICAL_MIX * sea_float * (state[..., 1:, :, :] - state[..., :-1, :, :])
    zero_layer = jnp.zeros_like(state[..., :1, :, :])
    change = (
        change
        + jnp.concatenate([vertical, zero_layer], -3)
        - jnp.concatenate([zero_layer, vertical], -3)
    )
    stepped = state + change + AGE_RATE * sea_float
    surface = stepped[..., :1, :, :] * (1.0 - SURFACE_RELAX * sea_float)
    return jnp.concatenate([surface, stepped[..., 1:, :, :]], -3)


def projection(running_number):
    row_index = jnp.arange(running_number)[:, None]
    column_index = jnp.arange(running_number - 1)[None, :]
    count_root = math.sqrt(running_number)
    interior = (row_index == column_index).astype(jnp.float32) - 1.0 / (
        running_number * (1.0 / count_root + 1.0)
    )
    return jnp.where(row_index == running_number - 1, -1.0 / count_root, interior)


def stacked_rows(globally_measured, observed_value, error_variance, live_slot, projector):
    running_number = globally_measured.shape[0]
    member_mean = jnp.sum(globally_measured, 0) / running_number
    innovation = observed_value - member_mean
    scaled = jnp.where(live_slot, 1.0 / jnp.sqrt(error_variance), 0.0)
    projected = jnp.dot(projector.T, globally_measured, precision=HIGHEST)
    return jnp.concatenate([projected, innovation[None, :]], 0) * scaled[None, :]


def invert_upper(leading):
    order = leading.shape[0]
    padded_order = 1 << max(order - 1, 1).bit_length()
    extra = padded_order - order
    filled = jnp.pad(leading, ((0, extra), (0, extra)))
    filled = filled + jnp.diag(
        jnp.concatenate([jnp.zeros((order,), jnp.float32), jnp.ones((extra,), jnp.float32)])
    )
    row_index = jnp.arange(padded_order)[:, None]
    column_index = jnp.arange(padded_order)[None, :]
    inverse = jnp.diag(1.0 / jnp.diagonal(filled))
    width = 1
    while width < padded_order:
        coupling = jnp.logical_and(
            row_index // (2 * width) == column_index // (2 * width),
            row_index // width < column_index // width,
        )
        linking = jnp.where(coupling, filled, 0.0)
        inverse = inverse - jnp.dot(
            jnp.dot(inverse, linking, precision=HIGHEST), inverse, precision=HIGHEST
        )
        width = width * 2
    return inverse[:order, :order]


def mixing_matrix(triangle, projector):
    running_number = triangle.shape[0]
    leading = triangle[: running_number - 1, : running_number - 1]
    carry_q = triangle[: running_number - 1, running_number - 1]
    inverse = invert_upper(leading)
    weights = jnp.dot(inverse, carry_q, precision=HIGHEST)
    spread = math.sqrt(running_number - 1) * jnp.dot(
        jnp.dot(projector, inverse, precision=HIGHEST), projector.T, precision=HIGHEST
    )
    return 1.0 / running_number + jnp.dot(projector, weights, precision=HIGHEST)[:, None] + spread


def per_device(
    background_elapsed_years,
    currents,
    diffusivity,
    sea_mask,
    observed_cell,
    measured_layer_number,
    live_counts,
    observed_value,
    error_variance,
):
    levels = background_elapsed_years.shape[1]
    sea_float = sea_mask.astype(jnp.float32)
    static = jnp.concatenate([currents[1], diffusivity, sea_float[None]], 0)
    padded_static = padded_2(static, (("grid", 1),), 1)
    north_speed = padded_static[:levels]
    padded_kappa = padded_static[levels : 2 * levels]
    padded_sea = padded_static[2 * levels]
    state = background_elapsed_years
    for step_index in range(STEPS):
        padded = padded_2(state, (("grid", 2),), 1)
        state = advance(
            state,
            padded,
            currents[0],
            diffusivity,
            north_speed,
            padded_kappa,
            sea_float,
            padded_sea,
        )
    own_members = state.shape[0]
    unrolled_array = state.reshape(own_members, -1)
    position = measured_layer_number * (state.shape[2] * state.shape[3]) + observed_cell
    local_seen = jnp.take(unrolled_array, position, axis=1)
    globally_measured = lax.all_gather(local_seen, "mem", axis=0, tiled=True)
    running_number = globally_measured.shape[0]
    projector = projection(running_number)
    live_slot = jnp.arange(observed_cell.shape[0]) < live_counts[0]
    stacked = stacked_rows(globally_measured, observed_value, error_variance, live_slot, projector)
    local_gram = jnp.dot(stacked, stacked.T, precision=HIGHEST)
    identity = jnp.eye(running_number, dtype=jnp.float32)
    gram_total = lax.psum(local_gram, "grid") + (running_number - 1) * identity
    first_factor = jnp.linalg.cholesky(gram_total).T
    mixing = mixing_matrix(first_factor, projector)
    layered = state.reshape(own_members, levels, -1)
    combined = jnp.einsum(
        "ki,klc->ilc",
        mixing,
        lax.all_to_all(layered, "mem", split_axis=2, concat_axis=0, tiled=True),
        precision=HIGHEST,
    )
    updated = lax.all_to_all(combined, "mem", split_axis=0, concat_axis=2, tiled=True)
    return updated.reshape(background_elapsed_years.shape)


def solution(mesh):
    placed = (
        P("mem", None, "grid", None),
        P(None, None, "grid", None),
        P(None, "grid", None),
        P("grid", None),
        P("grid"),
        P("grid"),
        P("grid"),
        P("grid"),
        P("grid"),
    )
    return jax.shard_map(
        per_device,
        mesh=mesh,
        in_specs=placed,
        out_specs=P("mem", None, "grid", None),
        check_vma=False,
    )
```

profile of v0, /device:TPU:1, one launch (start us, length us, event | category | flops | bytes accessed | tf_op | source)
XLA Modules:
  0.0 383.1 jit_solution(3219183451220257531)
XLA Ops:
  7.7 4.8 %collective-permute-start.2 = (f32[16,4,1,1440]{3,0,2,1:T(8,128)S(1)}, f32[16,4,1,1440]{3,0,2,1:T(8,128)S(1)}, u32[]{:S(2)}, u32[]{:S(2)}) collective-permute-start(f32[16,4,1,1440]{3,0,2,1:T(8,128)S(1)} %copy.113), channel_id=1, source_target_pairs={{0,8},{8,16},{16,24},{24,32},{32,40},{40,48},{48,56},{56,64},{64,7... | collective-permute-start | bytes 1105928 | tf_op jit(solution)/shard_map/ppermute | solution.py:24
  12.6 1.3 collective-permute-start.3
  17.1 1.3 collective-permute-start.1
  18.4 5.2 %collective-permute-start = (f32[9,1,1440]{2,1,0:T(1,128)S(1)}, f32[9,1,1440]{2,1,0:T(1,128)S(1)}, u32[]{:S(2)}, u32[]{:S(2)}) collective-permute-start(f32[9,1,1440]{2,1,0:T(1,128)S(1)} %pad_maximum_fusion.11), channel_id=1, source_target_pairs={{0,8},{8,16},{16,24},{24,32},{32,40},{40,48},{48,56},{56,64},{64,7... | collective-permute-start | bytes 155528 | tf_op jit(solution)/shard_map/ppermute | solution.py:24
  25.8 1.4 subtract_reduce_fusion
  32.1 1.3 collective-permute-start.5
  33.4 4.7 %collective-permute-start.4 = (f32[16,4,1,1440]{3,0,2,1:T(8,128)S(1)}, f32[16,4,1,1440]{3,0,2,1:T(8,128)S(1)}, u32[]{:S(2)}, u32[]{:S(2)}) collective-permute-start(f32[16,4,1,1440]{3,0,2,1:T(8,128)S(1)} %get-tuple-element.20), channel_id=1, source_target_pairs={{0,8},{8,16},{16,24},{24,32},{32,40},{40,48},{48,56},{56,64},{64,7... | collective-permute-start | bytes 1105928 | tf_op jit(solution)/shard_map/ppermute | solution.py:24
  38.1 3.1 collective-permute-done.5
  41.2 1.5 collective-permute-done.4
  43.5 1.3 collective-permute-start.7
  44.8 5.9 %collective-permute-start.6 = (f32[16,4,1,1440]{3,0,2,1:T(8,128)S(1)}, f32[16,4,1,1440]{3,0,2,1:T(8,128)S(1)}, u32[]{:S(2)}, u32[]{:S(2)}) collective-permute-start(f32[16,4,1,1440]{3,0,2,1:T(8,128)S(1)} %get-tuple-element.18), channel_id=1, source_target_pairs={{0,8},{8,16},{16,24},{24,32},{32,40},{40,48},{48,56},{56,64},{64,7... | collective-permute-start | bytes 1105928 | tf_op jit(solution)/shard_map/ppermute | solution.py:24
  50.8 3.1 collective-permute-done.7
  53.9 1.5 collective-permute-done.6
  56.1 1.3 collective-permute-start.9
  57.4 6.8 %collective-permute-start.8 = (f32[16,4,1,1440]{3,0,2,1:T(8,128)S(1)}, f32[16,4,1,1440]{3,0,2,1:T(8,128)S(1)}, u32[]{:S(2)}, u32[]{:S(2)}) collective-permute-start(f32[16,4,1,1440]{3,0,2,1:T(8,128)S(1)} %get-tuple-element.16), channel_id=1, source_target_pairs={{0,8},{8,16},{16,24},{24,32},{32,40},{40,48},{48,56},{56,64},{64,7... | collective-permute-start | bytes 1105928 | tf_op jit(solution)/shard_map/ppermute | solution.py:24
  64.4 3.1 collective-permute-done.9
  67.5 1.5 collective-permute-done.8
  69.5 2.1 copy.114
  71.6 1.9 copy.127
  73.5 2.9 gather_fusion
  76.6 19.5 %all_gather.3 = f32[128,512]{1,0:T(8,128)S(1)} all-gather(f32[16,512]{1,0:T(8,128)S(1)} %copy.115), channel_id=1, replica_groups=mesh['grid'=96,'mem'=8] {'mem'}, dimensions={0}, use_global_device_ids=true | all-gather | bytes 294912 | tf_op jit(solution)/shard_map/all_gather | solution.py:156
  97.7 1.7 bitcast_bitcast_fusion
  99.4 4.5 %reshape.1298 = f32[8,1,11520]{2,1,0:T(1,128)} reshape(f32[1440,4,16]{2,1,0:T(4,128)} %bitcast_bitcast_fusion) | data formatting | bytes 737280
  103.9 3.8 %all-to-all-start = ((f32[8,1,11520]{2,1,0:T(1,128)}), f32[8,1,11520]{2,1,0:T(1,128)S(1)}, u32[]{:S(2)}, u32[]{:S(2)}) async-start(f32[8,1,11520]{2,1,0:T(1,128)} %reshape.1298), calls=%async_computation | async-start | bytes 737280 | tf_op jit(solution)/shard_map/all_to_all | solution.py:170
  107.8 216.1 %all-reduce.11.cloned.1.call-done = f32[128,128]{0,1:T(8,128)} async-done(((f32[128,128]{0,1:T(8,128)}), f32[128,128]{0,1:T(8,128)}) %all-reduce.11.cloned.1.call-update) | async-done | bytes 65552 | tf_op jit(solution)/shard_map/psum | solution.py:163
  325.6 11.7 %cholesky.13 = f32[128,128]{1,0:T(8,128)S(1)} custom-call(f32[128,128]{1,0:T(8,128)S(1)} %fusion.47), custom_call_target="Cholesky" | custom-call | tf_op jit(solution)/shard_map/jit(cholesky)/cholesky | solution.py:164
  338.9 1.3 gather_fusion.1
  346.1 1.5 reduce.14
  347.6 2.0 reshape.1299
  349.6 2.6 copy.128
  353.5 20.5 %all_to_all.33 = f32[128,4,180]{2,1,0:T(4,128)S(1)} all-to-all(f32[128,4,180]{2,1,0:T(4,128)S(1)} %copy.130), channel_id=1, replica_groups=mesh['grid'=96,'mem'=8] {'mem'}, dimensions={0} | all-to-all | bytes 737280 | tf_op jit(solution)/shard_map/all_to_all | solution.py:173
  374.4 1.9 reshape.1293
  (120 shorter events, 25.4 us)
Async XLA Ops:
  6.5 24.2 %copy-start = (f32[16,4,1,1440]{3,2,1,0:T(1,128)S(1)}, f32[16,4,1,1440]{3,2,1,0:T(1,128)}, u32[]{:S(2)}) copy-start(f32[16,4,1,1440]{3,2,1,0:T(1,128)} %param.9) | copy-start | bytes 1105924
  6.5 23.9 %copy-start.1 = (f32[4,1,1440]{2,1,0:T(1,128)S(1)}, f32[4,1,1440]{2,1,0:T(1,128)}, u32[]{:S(2)}) copy-start(f32[4,1,1440]{2,1,0:T(1,128)} %param.11) | copy-start | bytes 69124
  6.5 317.3 %all-reduce.11.cloned.1.call-start = ((), (), s32[]{:S(2)}) async-start(), calls=%async_computation.2 | async-start | bytes 131072 | tf_op jit(solution)/shard_map/psum | solution.py:163
  7.7 23.0 %collective-permute-start.2 = (f32[16,4,1,1440]{3,0,2,1:T(8,128)S(1)}, f32[16,4,1,1440]{3,0,2,1:T(8,128)S(1)}, u32[]{:S(2)}, u32[]{:S(2)}) collective-permute-start(f32[16,4,1,1440]{3,0,2,1:T(8,128)S(1)} %copy.113), channel_id=1, source_target_pairs={{0,8},{8,16},{16,24},{24,32},{32,40},{40,48},{48,56},{56,64},{64,7... | collective-permute-start | bytes 1105928 | tf_op jit(solution)/shard_map/ppermute | solution.py:24
  12.6 18.5 %collective-permute-start.3 = (f32[16,4,1,1440]{3,0,2,1:T(8,128)S(1)}, f32[16,4,1,1440]{3,0,2,1:T(8,128)S(1)}, u32[]{:S(2)}, u32[]{:S(2)}) collective-permute-start(f32[16,4,1,1440]{3,0,2,1:T(8,128)S(1)} %copy.113), channel_id=1, source_target_pairs={{8,0},{16,8},{24,16},{32,24},{40,32},{48,40},{56,48},{64,56},{72,6... | collective-permute-start | bytes 1105928 | tf_op jit(solution)/shard_map/ppermute | solution.py:25
  17.1 13.3 %collective-permute-start.1 = (f32[9,1,1440]{2,1,0:T(1,128)S(1)}, f32[9,1,1440]{2,1,0:T(1,128)S(1)}, u32[]{:S(2)}, u32[]{:S(2)}) collective-permute-start(f32[9,1,1440]{2,1,0:T(1,128)S(1)} %pad_maximum_fusion.11), channel_id=1, source_target_pairs={{8,0},{16,8},{24,16},{32,24},{40,32},{48,40},{56,48},{64,56},{72,6... | collective-permute-start | bytes 155528 | tf_op jit(solution)/shard_map/ppermute | solution.py:25
  18.4 12.0 %collective-permute-start = (f32[9,1,1440]{2,1,0:T(1,128)S(1)}, f32[9,1,1440]{2,1,0:T(1,128)S(1)}, u32[]{:S(2)}, u32[]{:S(2)}) collective-permute-start(f32[9,1,1440]{2,1,0:T(1,128)S(1)} %pad_maximum_fusion.11), channel_id=1, source_target_pairs={{0,8},{8,16},{16,24},{24,32},{32,40},{40,48},{48,56},{56,64},{64,7... | collective-permute-start | bytes 155528 | tf_op jit(solution)/shard_map/ppermute | solution.py:24
  32.1 9.2 %collective-permute-start.5 = (f32[16,4,1,1440]{3,0,2,1:T(8,128)S(1)}, f32[16,4,1,1440]{3,0,2,1:T(8,128)S(1)}, u32[]{:S(2)}, u32[]{:S(2)}) collective-permute-start(f32[16,4,1,1440]{3,0,2,1:T(8,128)S(1)} %get-tuple-element.20), channel_id=1, source_target_pairs={{8,0},{16,8},{24,16},{32,24},{40,32},{48,40},{56,48},{64,56},{72,6... | collective-permute-start | bytes 1105928 | tf_op jit(solution)/shard_map/ppermute | solution.py:25
  33.4 9.3 %collective-permute-start.4 = (f32[16,4,1,1440]{3,0,2,1:T(8,128)S(1)}, f32[16,4,1,1440]{3,0,2,1:T(8,128)S(1)}, u32[]{:S(2)}, u32[]{:S(2)}) collective-permute-start(f32[16,4,1,1440]{3,0,2,1:T(8,128)S(1)} %get-tuple-element.20), channel_id=1, source_target_pairs={{0,8},{8,16},{16,24},{24,32},{32,40},{40,48},{48,56},{56,64},{64,7... | collective-permute-start | bytes 1105928 | tf_op jit(solution)/shard_map/ppermute | solution.py:24
  43.5 10.4 %collective-permute-start.7 = (f32[16,4,1,1440]{3,0,2,1:T(8,128)S(1)}, f32[16,4,1,1440]{3,0,2,1:T(8,128)S(1)}, u32[]{:S(2)}, u32[]{:S(2)}) collective-permute-start(f32[16,4,1,1440]{3,0,2,1:T(8,128)S(1)} %get-tuple-element.18), channel_id=1, source_target_pairs={{8,0},{16,8},{24,16},{32,24},{40,32},{48,40},{56,48},{64,56},{72,6... | collective-permute-start | bytes 1105928 | tf_op jit(solution)/shard_map/ppermute | solution.py:25
  44.8 10.5 %collective-permute-start.6 = (f32[16,4,1,1440]{3,0,2,1:T(8,128)S(1)}, f32[16,4,1,1440]{3,0,2,1:T(8,128)S(1)}, u32[]{:S(2)}, u32[]{:S(2)}) collective-permute-start(f32[16,4,1,1440]{3,0,2,1:T(8,128)S(1)} %get-tuple-element.18), channel_id=1, source_target_pairs={{0,8},{8,16},{16,24},{24,32},{32,40},{40,48},{48,56},{56,64},{64,7... | collective-permute-start | bytes 1105928 | tf_op jit(solution)/shard_map/ppermute | solution.py:24
  56.1 11.4 %collective-permute-start.9 = (f32[16,4,1,1440]{3,0,2,1:T(8,128)S(1)}, f32[16,4,1,1440]{3,0,2,1:T(8,128)S(1)}, u32[]{:S(2)}, u32[]{:S(2)}) collective-permute-start(f32[16,4,1,1440]{3,0,2,1:T(8,128)S(1)} %get-tuple-element.16), channel_id=1, source_target_pairs={{8,0},{16,8},{24,16},{32,24},{40,32},{48,40},{56,48},{64,56},{72,6... | collective-permute-start | bytes 1105928 | tf_op jit(solution)/shard_map/ppermute | solution.py:25
  57.4 11.5 %collective-permute-start.8 = (f32[16,4,1,1440]{3,0,2,1:T(8,128)S(1)}, f32[16,4,1,1440]{3,0,2,1:T(8,128)S(1)}, u32[]{:S(2)}, u32[]{:S(2)}) collective-permute-start(f32[16,4,1,1440]{3,0,2,1:T(8,128)S(1)} %get-tuple-element.16), channel_id=1, source_target_pairs={{0,8},{8,16},{16,24},{24,32},{32,40},{40,48},{48,56},{56,64},{64,7... | collective-permute-start | bytes 1105928 | tf_op jit(solution)/shard_map/ppermute | solution.py:24
  71.6 25.0 %copy-start.3 = (f32[512]{0:T(512)S(1)}, f32[512]{0:T(512)}, u32[]{:S(2)}) copy-start(f32[512]{0:T(512)} %param.16) | copy-start | bytes 6148
  99.4 239.4 %copy-start.2 = (f32[128]{0:T(128)S(1)}, f32[128]{0:T(128)}, u32[]{:S(2)}) copy-start(f32[128]{0:T(128)} %constant.279.clone.1) | copy-start | bytes 1540
  103.9 241.7 %all-to-all-start = ((f32[8,1,11520]{2,1,0:T(1,128)}), f32[8,1,11520]{2,1,0:T(1,128)S(1)}, u32[]{:S(2)}, u32[]{:S(2)}) async-start(f32[8,1,11520]{2,1,0:T(1,128)} %reshape.1298), calls=%async_computation | async-start | bytes 737280 | tf_op jit(solution)/shard_map/all_to_all | solution.py:170
Sparse Core Ops, SparseCore 0:
  97.8 225.9 all-reduce.10
where the time goes:
time: 384 us; the launch traced here: 383 us
  waiting for transfers between devices  230 us (60%)
  blocking collectives  40 us (10%)
  starting transfers between devices  37.7 us (10%)
  local copies, waits for them, and re-layouts  27 us (7%)
  other arithmetic  25.9 us (7%)
  between operations  14.7 us (4%)
  matrix products  7.82 us (2%)
    psum x1, waiting for transfers between devices, per_device(): gram_total = lax.psum(local_gram, 'grid') + (running_number - 1) * identity  216 us
    ppermute x5, starting transfers between devices, padded_2(): before = lax.ppermute(last, axis, up)  27.4 us
    all_to_all x1, blocking collectives, per_device(): lax.all_to_all(combined, 'mem', split_axis=0, concat_axis=2, tiled=True)  20.5 us
    all_gather x1, blocking collectives, per_device(): globally_measured = lax.all_gather(local_seen, 'mem', axis=0, tiled=True)  19.5 us
    another operation x3, other arithmetic, per_device(): first_factor = jnp.linalg.cholesky(gram_total).T  12.5 us
    unnamed x16, local copies, waits for them, and re-layouts  9.5 us
    ppermute x5, waiting for transfers between devices, padded_2(): after = lax.ppermute(leading, axis, down)  9.27 us
  transfers between devices with their start and end apart: 12, of which 7 were waited for; matrix products, arithmetic and copies ran while one was open for 10% of the time, Pallas kernels for 0%

commit v1 on v0

v1 whole, which is shorter than its diff:
```python
import functools
import math

import jax
import jax.numpy as jnp
from jax import lax
from jax.experimental import pallas as pl
from jax.experimental.pallas import tpu as pltpu
from jax.sharding import PartitionSpec as P

STEPS = 4
Z_RING = 12
LANES = 128
PANEL = 32
VERTICAL_MIX = 0.05
AGE_RATE = 0.25
SURFACE_RELAX = 0.5
HIGHEST = lax.Precision.HIGHEST
MESH = pl.DeviceIdType.MESH


def faces(speed_a, speed_b, kappa_a, kappa_b, sea_a, sea_b):
    speed = 0.5 * (speed_a + speed_b)
    kappa = 0.5 * (kappa_a + kappa_b)
    both = sea_a * sea_b
    return both * (jnp.maximum(speed, 0.0) + kappa), both * (jnp.minimum(speed, 0.0) - kappa)


def factor_inverse(gram, count):
    lane = lax.broadcasted_iota(jnp.int32, (PANEL, count), 1)
    row = lax.broadcasted_iota(jnp.int32, (PANEL, 1), 0)
    wide_row = lax.broadcasted_iota(jnp.int32, (PANEL, count), 0)
    full_row = lax.broadcasted_iota(jnp.int32, (count, count), 0)
    full_lane = lax.broadcasted_iota(jnp.int32, (count, count), 1)
    left = gram + jnp.where(full_row == full_lane, float(count - 1), 0.0)
    right = jnp.where(full_row == full_lane, 1.0, 0.0)
    done = []
    for first in range(0, count, PANEL):
        a, e = left[:PANEL], right[:PANEL]
        for k in range(PANEL):
            at = first + k
            scale = 1.0 / a[k : k + 1, at : at + 1]
            factor = jnp.where(row > k, a[:, at : at + 1] * scale, 0.0)
            a = a - factor * a[k : k + 1]
            e = e - factor * e[k : k + 1]
        pivots = jnp.sum(jnp.where(lane == wide_row + first, a, 0.0), axis=1, keepdims=True)
        root = lax.rsqrt(pivots)
        a, e = a * root, e * root
        done.append(e)
        if first + PANEL < count:
            turned = jnp.transpose(a)[first + PANEL :]
            left = left[PANEL:] - jnp.dot(turned, a, precision=HIGHEST)
            right = right[PANEL:] - jnp.dot(turned, e, precision=HIGHEST)
    return jnp.concatenate(done, 0)


def kernel(
    cfg,
    state_ref, vk_ref, us_ref, sea_ref, cell_ref, level_ref, live_ref, value_ref, variance_ref,
    out_ref,
    states, from_south, from_north, vk_south, vk_north, sea_south, sea_north,
    coefs, units, own_all, picks, part, slice_parts, z_own, z_parts, y_own, y_parts, total, gram, mixed,
    s_halo, r_halo, s_static, r_static, s_out, r_out, s_slice, r_slice, s_z, r_z, s_y, r_y, s_all, r_all, s_back, r_back,
):
    n_grid, n_mem, z_ring, levels, wide, chunks = cfg
    y_ring = n_grid // z_ring
    own = 8 * chunks
    count = n_mem * own
    unit_wide = levels * wide // n_mem
    halves = n_mem // levels
    grid = lax.axis_index("grid")
    mem = lax.axis_index("mem")
    y_at, z_at = grid // z_ring, lax.rem(grid, z_ring)
    has_north, has_south = grid < n_grid - 1, grid > 0

    def mem_peer(d):
        return lax.rem(mem + d, n_mem)

    def z_peer(d):
        return y_at * z_ring + lax.rem(z_at + d, z_ring)

    def y_peer(d):
        return lax.rem(y_at + d, y_ring) * z_ring + z_at

    barrier = pltpu.get_barrier_semaphore()

    def greet(where):
        pl.semaphore_signal(barrier, inc=1, device_id=where, device_id_type=MESH)

    cross_north = jnp.logical_and(has_north, z_at == z_ring - 1)
    cross_south = jnp.logical_and(has_south, z_at == 0)

    @pl.when(cross_north)
    def _():
        greet({"grid": grid + 1})

    @pl.when(cross_south)
    def _():
        greet({"grid": grid - 1})

    for d in range(1, z_ring):
        greet({"grid": z_peer(d)})
    for d in range(1, y_ring):
        greet({"grid": y_peer(d)})
    for d in range(1, n_mem):
        greet({"mem": mem_peer(d)})
    greeted = z_ring + y_ring + n_mem - 3 + cross_north.astype(jnp.int32) + cross_south.astype(jnp.int32)
    pl.semaphore_wait(barrier, greeted)

    def remote(src, dst, send, recv, where):
        return pltpu.make_async_remote_copy(
            src_ref=src, dst_ref=dst, send_sem=send, recv_sem=recv, device_id=where, device_id_type=MESH
        )

    north, south = {"grid": grid + 1}, {"grid": grid - 1}

    def halo(step, chunk):
        src = state_ref.at[chunk] if step == 0 else states.at[step - 1, chunk]
        up = remote(src, from_south.at[step, chunk], s_halo.at[0, step, chunk], r_halo.at[0, step, chunk], north)
        down = remote(src, from_north.at[step, chunk], s_halo.at[1, step, chunk], r_halo.at[1, step, chunk], south)
        return up, down

    static_up = (
        remote(vk_ref, vk_south, s_static.at[0, 0], r_static.at[0, 0], north),
        remote(sea_ref, sea_south, s_static.at[0, 1], r_static.at[0, 1], north),
    )
    static_down = (
        remote(vk_ref, vk_north, s_static.at[1, 0], r_static.at[1, 0], south),
        remote(sea_ref, sea_north, s_static.at[1, 1], r_static.at[1, 1], south),
    )

    def start_halo(step, chunk):
        up, down = halo(step, chunk)
        pl.when(has_north)(up.start)
        pl.when(has_south)(down.start)

    for copy in static_up:
        pl.when(has_north)(copy.start)
    for copy in static_down:
        pl.when(has_south)(copy.start)
    for chunk in range(chunks):
        start_halo(0, chunk)

    @pl.when(jnp.logical_not(has_south))
    def _():
        vk_south[...] = jnp.zeros_like(vk_south)
        sea_south[...] = jnp.zeros_like(sea_south)
        from_south[...] = jnp.zeros_like(from_south)

    @pl.when(jnp.logical_not(has_north))
    def _():
        vk_north[...] = jnp.zeros_like(vk_north)
        sea_north[...] = jnp.zeros_like(sea_north)
        from_north[...] = jnp.zeros_like(from_north)

    slots = cell_ref.shape[1]
    place = level_ref[...] * wide + cell_ref[...] - mem * unit_wide
    inside = jnp.logical_and(place >= 0, place < unit_wide)
    live = lax.broadcasted_iota(jnp.int32, (1, slots), 1) < live_ref[...]
    weight = jnp.where(jnp.logical_and(inside, live), 1.0 / jnp.sqrt(variance_ref[...]), 0.0)
    picks[...] = jnp.where(
        lax.broadcasted_iota(jnp.int32, (unit_wide, slots), 0) == place, 1.0, 0.0
    ).astype(jnp.bfloat16)

    velocity, kappa = vk_ref[0:levels], vk_ref[levels : 2 * levels]
    zonal = us_ref[0:levels]
    sea = jnp.broadcast_to(sea_ref[...], (levels, wide))
    a_east, b_east = faces(
        zonal, pltpu.roll(zonal, wide - 1, 1), kappa, pltpu.roll(kappa, wide - 1, 1), sea, pltpu.roll(sea, wide - 1, 1)
    )
    a_west, b_west = pltpu.roll(a_east, 1, 1), pltpu.roll(b_east, 1, 1)

    for copy in static_up:
        pl.when(has_south)(copy.wait_recv)
    for copy in static_down:
        pl.when(has_north)(copy.wait_recv)
    a_north, b_north = faces(
        velocity, vk_north[0:levels], kappa, vk_north[levels : 2 * levels], sea,
        jnp.broadcast_to(sea_north[...], (levels, wide)),
    )
    a_south, b_south = faces(
        vk_south[0:levels], velocity, vk_south[levels : 2 * levels], kappa,
        jnp.broadcast_to(sea_south[...], (levels, wide)), sea,
    )
    depth = lax.broadcasted_iota(jnp.int32, (levels, wide), 0)
    vertical = VERTICAL_MIX * sea
    borders = jnp.where(jnp.logical_or(depth == 0, depth == levels - 1), 1.0, 2.0)
    relax = jnp.where(depth == 0, 1.0 - SURFACE_RELAX * sea, 1.0)
    centre = 1.0 - a_east + b_west - a_north + b_south - borders * vertical
    parts = (centre, -b_east, a_west, -b_north, a_south, vertical, AGE_RATE * sea)
    for index, values in enumerate(parts):
        values = values * relax
        for level in range(levels):
            coefs[level, index] = jnp.broadcast_to(values[level : level + 1], (8, wide))

    for step in range(STEPS):
        for chunk in range(chunks):
            up, down = halo(step, chunk)
            pl.when(has_south)(up.wait_recv)
            pl.when(has_north)(down.wait_recv)
            for level in range(levels):
                def at(which):
                    return state_ref[chunk, which] if step == 0 else states[step - 1, chunk, which]

                here = at(level)
                around = at(level - 1) if level > 0 else 0.0
                if level < levels - 1:
                    around = around + at(level + 1)
                result = (
                    coefs[level, 0] * here
                    + coefs[level, 1] * pltpu.roll(here, wide - 1, 1)
                    + coefs[level, 2] * pltpu.roll(here, 1, 1)
                    + coefs[level, 3] * from_north[step, chunk, level]
                    + coefs[level, 4] * from_south[step, chunk, level]
                    + coefs[level, 5] * around
                    + coefs[level, 6]
                )
                if step < STEPS - 1:
                    states[step, chunk, level] = result
                else:
                    for half in range(halves):
                        units[level * halves + half, chunk] = result[:, half * unit_wide : (half + 1) * unit_wide]
            if step < STEPS - 1:
                start_halo(step + 1, chunk)
            else:
                rows = pl.ds(pl.multiple_of(mem * own + 8 * chunk, 8), 8)
                for d in range(1, n_mem):
                    remote(
                        units.at[mem_peer(d), chunk], own_all.at[rows], s_out.at[d - 1, chunk], r_out.at[d - 1, chunk],
                        {"mem": mem_peer(d)},
                    ).start()
                own_all[rows, :] = units[mem, chunk]

    def exchange(src_of, dst_of, send, recv, peers, axis, peer):
        return [remote(src_of(d), dst_of(d), send.at[d - 1], recv.at[d - 1], {axis: peer(d)}) for d in range(1, peers)]

    outs = [
        remote(
            units.at[mem_peer(d), chunk],
            own_all.at[pl.ds(pl.multiple_of(mem * own + 8 * chunk, 8), 8)],
            s_out.at[d - 1, chunk], r_out.at[d - 1, chunk], {"mem": mem_peer(d)},
        )
        for d in range(1, n_mem)
        for chunk in range(chunks)
    ]
    for copy in outs:
        copy.wait_recv()

    fields = own_all[...]
    high = fields.astype(jnp.bfloat16)
    rest = fields - high.astype(jnp.float32)
    middle = rest.astype(jnp.bfloat16)
    low = (rest - middle.astype(jnp.float32)).astype(jnp.bfloat16)
    seen = (
        jnp.dot(high, picks[...], preferred_element_type=jnp.float32)
        + jnp.dot(middle, picks[...], preferred_element_type=jnp.float32)
        + jnp.dot(low, picks[...], preferred_element_type=jnp.float32)
    )
    root = math.sqrt(count)
    inner = 1.0 / (count * (1.0 / root + 1.0))
    last = lax.broadcasted_iota(jnp.int32, (count, slots), 0) == count - 1
    everyone = jnp.sum(seen, axis=0, keepdims=True)
    final = seen[count - 1 : count]
    shared = -inner * (everyone - final) - final / root
    stacked = jnp.where(last, value_ref[...] - everyone / count, seen + shared) * weight
    part[...] = lax.dot_general(
        stacked, stacked, (((1,), (1,)), ((), ())), precision=HIGHEST, preferred_element_type=jnp.float32
    ).reshape(n_mem, own, count)

    slices = exchange(lambda d: part.at[mem_peer(d)], lambda d: slice_parts.at[d - 1], s_slice, r_slice, n_mem, "mem", mem_peer)
    for copy in slices:
        copy.start()
    for copy in slices:
        copy.wait_recv()
    z_own[...] = part[mem] + jnp.sum(slice_parts[...], axis=0)
    along_z = exchange(lambda d: z_own, lambda d: z_parts.at[d - 1], s_z, r_z, z_ring, "grid", z_peer)
    for copy in along_z:
        copy.start()
    for copy in along_z:
        copy.wait_recv()
    y_own[...] = z_own[...] + jnp.sum(z_parts[...], axis=0)
    along_y = exchange(lambda d: y_own, lambda d: y_parts.at[d - 1], s_y, r_y, y_ring, "grid", y_peer)
    for copy in along_y:
        copy.start()
    for copy in along_y:
        copy.wait_recv()
    total[...] = y_own[...] + jnp.sum(y_parts[...], axis=0)
    gathered = exchange(lambda d: total, lambda d: gram.at[mem], s_all, r_all, n_mem, "mem", mem_peer)
    for copy in gathered:
        copy.start()
    gram[mem] = total[...]
    for copy in gathered:
        copy.wait_recv()

    inverse = factor_inverse(gram[...].reshape(count, count), count)
    square_lane = lax.broadcasted_iota(jnp.int32, (count, count), 1)
    square_row = lax.broadcasted_iota(jnp.int32, (count, count), 0)
    leading = jnp.where(square_lane < count - 1, inverse, 0.0)
    across = jnp.sum(leading, axis=1, keepdims=True)
    turned = jnp.where(square_lane == count - 1, -across / root, leading - inner * across)
    shift = -turned[count - 1 : count] / inverse[count - 1 : count, count - 1 : count]
    kept = jnp.where(square_row < count - 1, turned, 0.0)
    down_sum = jnp.sum(kept, axis=0, keepdims=True)
    spread = jnp.where(square_row == count - 1, -down_sum / root, kept - inner * down_sum)
    mixing = 1.0 / count + shift + math.sqrt(count - 1) * spread
    mixed[...] = jnp.dot(mixing, own_all[...], precision=HIGHEST).reshape(n_mem, own, unit_wide)
    back = exchange(lambda d: mixed.at[mem_peer(d)], lambda d: out_ref.at[mem], s_back, r_back, n_mem, "mem", mem_peer)
    for copy in back:
        copy.start()
    out_ref[mem] = mixed[mem]
    for copy in back:
        copy.wait_recv()

    for step in range(STEPS):
        for chunk in range(chunks):
            up, down = halo(step, chunk)
            pl.when(has_north)(up.wait_send)
            pl.when(has_south)(down.wait_send)
    for copy in static_up:
        pl.when(has_north)(copy.wait_send)
    for copy in static_down:
        pl.when(has_south)(copy.wait_send)
    for copy in outs + slices + along_z + along_y + gathered + back:
        copy.wait_send()


def ring(x, wide):
    lon = x.shape[-1]
    gap = jnp.zeros(x.shape[:-1] + (wide - lon - 2 * STEPS,), x.dtype)
    return jnp.concatenate([x, x[..., :STEPS], gap, x[..., lon - STEPS :]], -1)


def per_device(
    n_grid, n_mem, z_ring,
    background_elapsed_years, currents, diffusivity, sea_mask, observed_cell, measured_layer_number, live_counts,
    observed_value, error_variance,
):
    own, levels, _, lon = background_elapsed_years.shape
    chunks, slots = own // 8, observed_cell.shape[0]
    halves = n_mem // levels
    block = LANES * halves
    wide = -(-(lon + 2 * STEPS) // block) * block
    unit_wide = wide // halves
    y_ring = n_grid // z_ring
    count = own * n_mem
    state = ring(background_elapsed_years.reshape(chunks, 8, levels, lon).transpose(0, 2, 1, 3), wide)
    vk = ring(jnp.concatenate([currents[1, :, 0], diffusivity[:, 0]], 0), wide)
    us = ring(currents[0, :, 0], wide)
    sea = ring(sea_mask.astype(jnp.float32), wide)
    f32 = jnp.float32
    dma = pltpu.SemaphoreType.DMA
    halo_shape = (STEPS, chunks, levels, 8, wide)
    scratch = [
        pltpu.VMEM((STEPS - 1, chunks, levels, 8, wide), f32),
        pltpu.VMEM(halo_shape, f32),
        pltpu.VMEM(halo_shape, f32),
        pltpu.VMEM((2 * levels, wide), f32),
        pltpu.VMEM((2 * levels, wide), f32),
        pltpu.VMEM((1, wide), f32),
        pltpu.VMEM((1, wide), f32),
        pltpu.VMEM((levels, 7, 8, wide), f32),
        pltpu.VMEM((n_mem, chunks, 8, unit_wide), f32),
        pltpu.VMEM((count, unit_wide), f32),
        pltpu.VMEM((unit_wide, slots), jnp.bfloat16),
        pltpu.VMEM((n_mem, own, count), f32),
        pltpu.VMEM((n_mem - 1, own, count), f32),
        pltpu.VMEM((own, count), f32),
        pltpu.VMEM((z_ring - 1, own, count), f32),
        pltpu.VMEM((own, count), f32),
        pltpu.VMEM((y_ring - 1, own, count), f32),
        pltpu.VMEM((own, count), f32),
        pltpu.VMEM((n_mem, own, count), f32),
        pltpu.VMEM((n_mem, own, unit_wide), f32),
    ]
    semaphores = [
        dma((2, STEPS, chunks)), dma((2, STEPS, chunks)),
        dma((2, 2)), dma((2, 2)),
        dma((n_mem - 1, chunks)), dma((n_mem - 1, chunks)),
        dma((n_mem - 1,)), dma((n_mem - 1,)),
        dma((z_ring - 1,)), dma((z_ring - 1,)),
        dma((y_ring - 1,)), dma((y_ring - 1,)),
        dma((n_mem - 1,)), dma((n_mem - 1,)),
        dma((n_mem - 1,)), dma((n_mem - 1,)),
    ]
    vmem = pl.BlockSpec(memory_space=pltpu.VMEM)
    result = pl.pallas_call(
        functools.partial(kernel, (n_grid, n_mem, z_ring, levels, wide, chunks)),
        out_shape=jax.ShapeDtypeStruct((n_mem, own, unit_wide), f32),
        in_specs=[vmem] * 9,
        out_specs=vmem,
        scratch_shapes=scratch + semaphores,
        compiler_params=pltpu.CompilerParams(
            collective_id=0, has_side_effects=True, vmem_limit_bytes=40 * 1024 * 1024
        ),
    )(
        state, vk, us, sea, observed_cell[None], measured_layer_number[None], live_counts[None],
        observed_value[None], error_variance[None],
    )
    whole = result.reshape(levels, halves, own, unit_wide).transpose(2, 0, 1, 3).reshape(own, levels, wide)
    return whole[:, :, None, :lon]


def solution(mesh):
    placed = (
        P("mem", None, "grid", None),
        P(None, None, "grid", None),
        P(None, "grid", None),
        P("grid", None),
        P("grid"),
        P("grid"),
        P("grid"),
        P("grid"),
        P("grid"),
    )
    return jax.shard_map(
        functools.partial(per_device, mesh.shape["grid"], mesh.shape["mem"], Z_RING),
        mesh=mesh,
        in_specs=placed,
        out_specs=P("mem", None, "grid", None),
        check_vma=False,
    )
```

time: 384 us -> 109 us (0.28)
  waiting for transfers between devices: 230 us -> 0 us
  Pallas kernels: 0 us -> 102 us
  blocking collectives: 40 us -> 0 us
  starting transfers between devices: 37.7 us -> 0 us
  other arithmetic: 25.9 us -> 0.1 us
  local copies, waits for them, and re-layouts: 27 us -> 6.15 us
  between operations: 14.7 us -> 0.74 us
  matrix products: 7.82 us -> 0 us
    psum x1 -> x0, waiting for transfers between devices: 216 us -> none  [per_device(): gram_total = lax.psum(local_gram, 'grid') + (running_number - 1) * identity]
    pallas_call x0 -> x1, Pallas kernels: none -> 102 us  [per_device(): pl.pallas_call(functools.partial(kernel, (n_grid, n_mem, z_ring, levels,...]
    ppermute x10 -> x0, starting transfers between devices: 33.9 us -> none  [the longest x5 27.4 us: padded_2(): before = lax.ppermute(last, axis, up)]
    all_to_all x1 -> x0, blocking collectives: 20.5 us -> none  [per_device(): lax.all_to_all(combined, 'mem', split_axis=0, concat_axis=2, tiled=True)]
    all_gather x1 -> x0, blocking collectives: 19.5 us -> none  [per_device(): globally_measured = lax.all_gather(local_seen, 'mem', axis=0, tiled=True)]
    ppermute x10 -> x0, waiting for transfers between devices: 13.7 us -> none  [the longest x5 9.27 us: padded_2(): after = lax.ppermute(leading, axis, down)]
    another operation x3 -> x0, other arithmetic: 12.5 us -> none  [per_device(): first_factor = jnp.linalg.cholesky(gram_total).T]
    dot_general x21 -> x0, matrix products: 7.82 us -> none  [the longest x7 2.36 us: invert_upper(): jnp.dot(inverse, linking, precision=HIGHEST)]
  transfers between devices with their start and end apart: 12 -> 0, of which waited for: 7 -> 0; matrix products, arithmetic and copies ran while one was open for 10% -> 0% of each run, Pallas kernels for 0% -> 0%
where the time goes in v1:
time: 109 us
  Pallas kernels  102 us (94%)
  local copies, waits for them, and re-layouts  6.15 us (6%)
    pallas_call x1, Pallas kernels, per_device(): pl.pallas_call(functools.partial(kernel, (n_grid, n_mem, z_ring, levels,...  102 us
    unnamed x15, local copies, waits for them, and re-layouts  2.7 us

profile of v1, /device:TPU:1, one launch (start us, length us, event | category | flops | bytes accessed | tf_op | source)
XLA Modules:
  0.0 109.0 jit_solution(905389822260996335)
XLA Ops:
  0.0 1.1 %copy_bitcast_fusion = f32[2,4,8,1440]{3,2,1,0:T(8,128)S(1)} fusion(f32[16,4,1,1440]{3,2,1,0:T(1,128)} %param.9), kind=kLoop, calls=%fused_computation | loop fusion | bytes 737280 | tf_op jit(solution)/shard_map/transpose | solution.py:346
  1.1 0.1 fusion.2
  1.2 0.0 copy-start.5
  1.2 0.1 concatenate.15.state_ref
  1.3 0.6 copy-done.5
  1.9 0.0 copy-start.4
  2.0 0.8 copy-done.4
  2.8 0.1 fusion.1
  2.9 0.1 concatenate.17.vk_ref
  2.9 0.1 fusion.4
  3.0 0.0 copy-start.6
  3.0 0.1 concatenate.18.us_ref
  3.1 0.6 copy-done.6
  3.7 0.1 fusion.5
  3.8 0.0 copy-start.2
  3.8 0.0 copy-start.3
  3.8 0.1 concatenate.19.sea_ref
  4.6 0.0 copy-start.1
  4.6 0.0 copy-start
  4.6 0.0 copy-done.2
  4.6 0.0 copy-done.3
  4.6 0.6 copy-done.1
  5.2 0.0 copy-done
  5.3 102.0 %shard_map.91 = f32[8,16,768]{2,1,0:T(8,128)S(1)} custom-call(f32[2,4,8,1536]{3,2,1,0:T(8,128)S(1)} %concatenate.15.state_ref, f32[8,1536]{1,0:T(8,128)S(1)} %concatenate.17.vk_ref, f32[4,1536]{1,0:T(4,128)S(1)} %concatenate.18.us_ref, f32[1,1536]{1,0:T(1,128)S(1)} %concatenate.19.sea_ref, s32[1,512]{1,0:T(1,128)S(1)} %bitcast.23, s32[1,512]{1,0:T(1,128)S(1)} %bitcast.24, ...), custom_call_target="tpu_custom_call" | custom-call | tf_op jit(solution)/shard_map/pallas_call | solution.py:386
  107.3 0.3 copy.17
  107.6 0.4 reshape.11
  108.0 1.0 broadcast_in_dim.39
  (9 shorter events, 0.1 us)
Async XLA Ops:
  1.2 0.7 copy-start.5
  1.9 0.8 copy-start.4
  3.0 0.7 copy-start.6
  3.8 0.8 copy-start.2
  3.8 0.8 copy-start.3
  4.6 0.7 copy-start.1
  4.6 0.7 copy-start

commit v2 on v1

--- a/solution.py
+++ b/solution.py
@@ -11,7 +11,7 @@
 STEPS = 4
 Z_RING = 12
 LANES = 128
-PANEL = 32
+PANEL = 64
 VERTICAL_MIX = 0.05
 AGE_RATE = 0.25
 SURFACE_RELAX = 0.5
@@ -27,40 +27,74 @@
 
 
 def factor_inverse(gram, count):
-    lane = lax.broadcasted_iota(jnp.int32, (PANEL, count), 1)
-    row = lax.broadcasted_iota(jnp.int32, (PANEL, 1), 0)
-    wide_row = lax.broadcasted_iota(jnp.int32, (PANEL, count), 0)
+    panel = min(PANEL, count)
+    wide_row = lax.broadcasted_iota(jnp.int32, (panel, count), 0)
+    lane = lax.broadcasted_iota(jnp.int32, (panel, count), 1)
+    row = lax.broadcasted_iota(jnp.int32, (8, count), 0)
     full_row = lax.broadcasted_iota(jnp.int32, (count, count), 0)
     full_lane = lax.broadcasted_iota(jnp.int32, (count, count), 1)
     left = gram + jnp.where(full_row == full_lane, float(count - 1), 0.0)
     right = jnp.where(full_row == full_lane, 1.0, 0.0)
     done = []
-    for first in range(0, count, PANEL):
-        a, e = left[:PANEL], right[:PANEL]
-        for k in range(PANEL):
-            at = first + k
-            scale = 1.0 / a[k : k + 1, at : at + 1]
-            factor = jnp.where(row > k, a[:, at : at + 1] * scale, 0.0)
-            a = a - factor * a[k : k + 1]
-            e = e - factor * e[k : k + 1]
+    for first in range(0, count, panel):
+        a_rest, e_rest = left[:panel], right[:panel]
+        a_done, e_done = [], []
+        for base in range(first, first + panel, 8):
+            a, e, a_rest, e_rest = a_rest[:8], e_rest[:8], a_rest[8:], e_rest[8:]
+            columns = [jnp.broadcast_to(a[:, base + j : base + j + 1], (8, count)) for j in range(8)]
+            scales = []
+            for k in range(0, 8, 2):
+                now, later = columns[k], columns[k + 1]
+                p, q, r = now[k : k + 1], now[k + 1 : k + 2], later[k + 1 : k + 2]
+                per_pair, per_p = 1.0 / (p * r - q * q), 1.0 / p
+                below_now, below_later = jnp.where(row > k + 1, now, 0.0), jnp.where(row > k + 1, later, 0.0)
+                first_factor = (below_now * r - below_later * q) * per_pair
+                later_factor = (below_later * p - below_now * q) * per_pair
+                first_factor = jnp.where(row == k + 1, q * per_p, first_factor)
+                for j in range(k + 2, 8):
+                    at = columns[j]
+                    columns[j] = at - (first_factor * at[k : k + 1] + later_factor * at[k + 1 : k + 2])
+                a = a - (first_factor * a[k : k + 1] + later_factor * a[k + 1 : k + 2])
+                e = e - (first_factor * e[k : k + 1] + later_factor * e[k + 1 : k + 2])
+                scales += [per_p, per_pair * p]
+            a_done.append(a)
+            e_done.append(e)
+            rows = first + panel - base - 8
+            if rows:
+                lower = [jnp.broadcast_to(a_rest[:, base + j : base + j + 1], (rows, count)) for j in range(8)]
+                for k in range(8):
+                    factor = lower[k] * scales[k]
+                    for j in range(k + 1, 8):
+                        lower[j] = lower[j] - factor * columns[j][k : k + 1]
+                    a_rest = a_rest - factor * a[k : k + 1]
+                    e_rest = e_rest - factor * e[k : k + 1]
+        a, e = jnp.concatenate(a_done, 0), jnp.concatenate(e_done, 0)
         pivots = jnp.sum(jnp.where(lane == wide_row + first, a, 0.0), axis=1, keepdims=True)
         root = lax.rsqrt(pivots)
         a, e = a * root, e * root
         done.append(e)
-        if first + PANEL < count:
-            turned = jnp.transpose(a)[first + PANEL :]
-            left = left[PANEL:] - jnp.dot(turned, a, precision=HIGHEST)
-            right = right[PANEL:] - jnp.dot(turned, e, precision=HIGHEST)
+        if first + panel < count:
+            turned = jnp.transpose(a)[first + panel :]
+            left = left[panel:] - jnp.dot(turned, a, precision=HIGHEST)
+            right = right[panel:] - jnp.dot(turned, e, precision=HIGHEST)
     return jnp.concatenate(done, 0)
+
+
+def ring(x, wide):
+    rows, lon = x.shape
+    gap = jnp.zeros((rows, wide - lon - 2 * STEPS), x.dtype)
+    return jnp.concatenate([x, x[:, :STEPS], gap, x[:, lon - STEPS :]], 1)
 
 
 def kernel(
     cfg,
-    state_ref, vk_ref, us_ref, sea_ref, cell_ref, level_ref, live_ref, value_ref, variance_ref,
+    first_hbm, currents_hbm, kappa_hbm, mask_hbm, cell_hbm, level_hbm, live_hbm, value_hbm, variance_hbm,
     out_ref,
-    states, from_south, from_north, vk_south, vk_north, sea_south, sea_north,
-    coefs, units, own_all, picks, part, slice_parts, z_own, z_parts, y_own, y_parts, total, gram, mixed,
-    s_halo, r_halo, s_static, r_static, s_out, r_out, s_slice, r_slice, s_z, r_z, s_y, r_y, s_all, r_all, s_back, r_back,
+    first_ref, currents_ref, kappa_ref, mask_ref, cell_ref, level_ref, live_ref, value_ref, variance_ref,
+    states, raw_south, raw_north, from_south, from_north, v_south, v_north, k_south, k_north, mask_south, mask_north,
+    coefs, units, own_all, picks, part, slice_parts, y_own, y_parts, z_own, z_parts, total, gram, mixed, landed, final_ref,
+    s_in, s_halo, r_halo, s_static, r_static, s_out, r_out, s_slice, r_slice, s_z, r_z, s_y, r_y,
+    s_all, r_all, s_back, r_back, s_leave,
 ):
     n_grid, n_mem, z_ring, levels, wide, chunks = cfg
     y_ring = n_grid // z_ring
@@ -82,6 +116,18 @@
     def y_peer(d):
         return lax.rem(y_at + d, y_ring) * z_ring + z_at
 
+    local = [
+        pltpu.make_async_copy(src, dst, s_in.at[index])
+        for index, (src, dst) in enumerate(
+            (
+                (first_hbm, first_ref), (currents_hbm, currents_ref), (kappa_hbm, kappa_ref), (mask_hbm, mask_ref),
+                (cell_hbm, cell_ref), (level_hbm, level_ref), (live_hbm, live_ref), (value_hbm, value_ref),
+                (variance_hbm, variance_ref),
+            )
+        )
+    ]
+    for copy in local:
+        copy.start()
     barrier = pltpu.get_barrier_semaphore()
 
     def greet(where):
@@ -98,7 +144,7 @@
     def _():
         greet({"grid": grid - 1})
 
-    for d in range(1, z_ring):
+    for d in sorted(range(1, z_ring), key=lambda d: min(d, z_ring - d)):
         greet({"grid": z_peer(d)})
     for d in range(1, y_ring):
         greet({"grid": y_peer(d)})
@@ -115,19 +161,24 @@
     north, south = {"grid": grid + 1}, {"grid": grid - 1}
 
     def halo(step, chunk):
-        src = state_ref.at[chunk] if step == 0 else states.at[step - 1, chunk]
-        up = remote(src, from_south.at[step, chunk], s_halo.at[0, step, chunk], r_halo.at[0, step, chunk], north)
-        down = remote(src, from_north.at[step, chunk], s_halo.at[1, step, chunk], r_halo.at[1, step, chunk], south)
+        if step == 0:
+            rows = pl.ds(8 * chunk, 8)
+            src, below, above = first_hbm.at[rows], raw_south.at[rows], raw_north.at[rows]
+        else:
+            src, below, above = states.at[step, chunk], from_south.at[step - 1, chunk], from_north.at[step - 1, chunk]
+        up = remote(src, below, s_halo.at[0, step, chunk], r_halo.at[0, step, chunk], north)
+        down = remote(src, above, s_halo.at[1, step, chunk], r_halo.at[1, step, chunk], south)
         return up, down
 
-    static_up = (
-        remote(vk_ref, vk_south, s_static.at[0, 0], r_static.at[0, 0], north),
-        remote(sea_ref, sea_south, s_static.at[0, 1], r_static.at[0, 1], north),
-    )
-    static_down = (
-        remote(vk_ref, vk_north, s_static.at[1, 0], r_static.at[1, 0], south),
-        remote(sea_ref, sea_north, s_static.at[1, 1], r_static.at[1, 1], south),
-    )
+    statics = (currents_hbm.at[1], kappa_hbm, mask_hbm)
+    static_up = [
+        remote(src, dst, s_static.at[0, index], r_static.at[0, index], north)
+        for index, (src, dst) in enumerate(zip(statics, (v_south, k_south, mask_south)))
+    ]
+    static_down = [
+        remote(src, dst, s_static.at[1, index], r_static.at[1, index], south)
+        for index, (src, dst) in enumerate(zip(statics, (v_north, k_north, mask_north)))
+    ]
 
     def start_halo(step, chunk):
         up, down = halo(step, chunk)
@@ -143,28 +194,45 @@
 
     @pl.when(jnp.logical_not(has_south))
     def _():
-        vk_south[...] = jnp.zeros_like(vk_south)
-        sea_south[...] = jnp.zeros_like(sea_south)
+        v_south[...] = jnp.zeros_like(v_south)
+        k_south[...] = jnp.zeros_like(k_south)
+        mask_south[...] = jnp.zeros_like(mask_south)
+        raw_south[...] = jnp.zeros_like(raw_south)
         from_south[...] = jnp.zeros_like(from_south)
 
     @pl.when(jnp.logical_not(has_north))
     def _():
-        vk_north[...] = jnp.zeros_like(vk_north)
-        sea_north[...] = jnp.zeros_like(sea_north)
+        v_north[...] = jnp.zeros_like(v_north)
+        k_north[...] = jnp.zeros_like(k_north)
+        mask_north[...] = jnp.zeros_like(mask_north)
+        raw_north[...] = jnp.zeros_like(raw_north)
         from_north[...] = jnp.zeros_like(from_north)
 
-    slots = cell_ref.shape[1]
-    place = level_ref[...] * wide + cell_ref[...] - mem * unit_wide
+    def first_rows(ref, chunk, level):
+        return ring(ref[8 * chunk : 8 * chunk + 8, level, 0, :], wide)
+
+    for copy in local:
+        copy.wait()
+    for chunk in range(chunks):
+        for level in range(levels):
+            states[0, chunk, level] = first_rows(first_ref, chunk, level)
+    slots = cell_ref.shape[0]
+    place = (level_ref[...] * wide + cell_ref[...]).reshape(1, slots) - mem * unit_wide
     inside = jnp.logical_and(place >= 0, place < unit_wide)
-    live = lax.broadcasted_iota(jnp.int32, (1, slots), 1) < live_ref[...]
-    weight = jnp.where(jnp.logical_and(inside, live), 1.0 / jnp.sqrt(variance_ref[...]), 0.0)
+    live = lax.broadcasted_iota(jnp.int32, (1, slots), 1) < live_ref[0]
+    weight = jnp.where(jnp.logical_and(inside, live), 1.0 / jnp.sqrt(variance_ref[...].reshape(1, slots)), 0.0)
     picks[...] = jnp.where(
         lax.broadcasted_iota(jnp.int32, (unit_wide, slots), 0) == place, 1.0, 0.0
     ).astype(jnp.bfloat16)
 
-    velocity, kappa = vk_ref[0:levels], vk_ref[levels : 2 * levels]
-    zonal = us_ref[0:levels]
-    sea = jnp.broadcast_to(sea_ref[...], (levels, wide))
+    def rows_of(ref):
+        return ring(ref[:, 0, :], wide)
+
+    def sea_of(ref):
+        return jnp.broadcast_to(ring(ref[...].astype(jnp.float32), wide), (levels, wide))
+
+    zonal, velocity = ring(currents_ref[0, :, 0, :], wide), ring(currents_ref[1, :, 0, :], wide)
+    kappa, sea = rows_of(kappa_ref), sea_of(mask_ref)
     a_east, b_east = faces(
         zonal, pltpu.roll(zonal, wide - 1, 1), kappa, pltpu.roll(kappa, wide - 1, 1), sea, pltpu.roll(sea, wide - 1, 1)
     )
@@ -174,14 +242,8 @@
         pl.when(has_south)(copy.wait_recv)
     for copy in static_down:
         pl.when(has_north)(copy.wait_recv)
-    a_north, b_north = faces(
-        velocity, vk_north[0:levels], kappa, vk_north[levels : 2 * levels], sea,
-        jnp.broadcast_to(sea_north[...], (levels, wide)),
-    )
-    a_south, b_south = faces(
-        vk_south[0:levels], velocity, vk_south[levels : 2 * levels], kappa,
-        jnp.broadcast_to(sea_south[...], (levels, wide)), sea,
-    )
+    a_north, b_north = faces(velocity, rows_of(v_north), kappa, rows_of(k_north), sea, sea_of(mask_north))
+    a_south, b_south = faces(rows_of(v_south), velocity, rows_of(k_south), kappa, sea_of(mask_south), sea)
     depth = lax.broadcasted_iota(jnp.int32, (levels, wide), 0)
     vertical = VERTICAL_MIX * sea
     borders = jnp.where(jnp.logical_or(depth == 0, depth == levels - 1), 1.0, 2.0)
@@ -200,8 +262,12 @@
             pl.when(has_north)(down.wait_recv)
             for level in range(levels):
                 def at(which):
-                    return state_ref[chunk, which] if step == 0 else states[step - 1, chunk, which]
-
+                    return states[step, chunk, which]
+
+                if step == 0:
+                    above, below = first_rows(raw_north, chunk, level), first_rows(raw_south, chunk, level)
+                else:
+                    above, below = from_north[step - 1, chunk, level], from_south[step - 1, chunk, level]
                 here = at(level)
                 around = at(level - 1) if level > 0 else 0.0
                 if level < levels - 1:
@@ -210,13 +276,13 @@
                     coefs[level, 0] * here
                     + coefs[level, 1] * pltpu.roll(here, wide - 1, 1)
                     + coefs[level, 2] * pltpu.roll(here, 1, 1)
-                    + coefs[level, 3] * from_north[step, chunk, level]
-                    + coefs[level, 4] * from_south[step, chunk, level]
+                    + coefs[level, 3] * above
+                    + coefs[level, 4] * below
                     + coefs[level, 5] * around
                     + coefs[level, 6]
                 )
                 if step < STEPS - 1:
-                    states[step, chunk, level] = result
+                    states[step + 1, chunk, level] = result
                 else:
                     for half in range(halves):
                         units[level * halves + half, chunk] = result[:, half * unit_wide : (half + 1) * unit_wide]
@@ -262,7 +328,7 @@
     everyone = jnp.sum(seen, axis=0, keepdims=True)
     final = seen[count - 1 : count]
     shared = -inner * (everyone - final) - final / root
-    stacked = jnp.where(last, value_ref[...] - everyone / count, seen + shared) * weight
+    stacked = jnp.where(last, value_ref[...].reshape(1, slots) - everyone / count, seen + shared) * weight
     part[...] = lax.dot_general(
         stacked, stacked, (((1,), (1,)), ((), ())), precision=HIGHEST, preferred_element_type=jnp.float32
     ).reshape(n_mem, own, count)
@@ -304,12 +370,22 @@
     spread = jnp.where(square_row == count - 1, -down_sum / root, kept - inner * down_sum)
     mixing = 1.0 / count + shift + math.sqrt(count - 1) * spread
     mixed[...] = jnp.dot(mixing, own_all[...], precision=HIGHEST).reshape(n_mem, own, unit_wide)
-    back = exchange(lambda d: mixed.at[mem_peer(d)], lambda d: out_ref.at[mem], s_back, r_back, n_mem, "mem", mem_peer)
+    mine = (
+        mem // halves,
+        slice(None),
+        pl.ds(pl.multiple_of(lax.rem(mem, halves) * unit_wide, LANES), unit_wide),
+    )
+    back = exchange(lambda d: mixed.at[mem_peer(d)], lambda d: landed.at[mine], s_back, r_back, n_mem, "mem", mem_peer)
     for copy in back:
         copy.start()
-    out_ref[mem] = mixed[mem]
+    landed[mine] = mixed[mem]
     for copy in back:
         copy.wait_recv()
+    leaving = []
+    for level in range(levels):
+        final_ref[level] = landed[level][:, : final_ref.shape[2]]
+        leaving.append(pltpu.make_async_copy(final_ref.at[level], out_ref.at[:, level, 0, :], s_leave.at[level]))
+        leaving[-1].start()
 
     for step in range(STEPS):
         for chunk in range(chunks):
@@ -320,14 +396,10 @@
         pl.when(has_north)(copy.wait_send)
     for copy in static_down:
         pl.when(has_south)(copy.wait_send)
+    for copy in leaving:
+        copy.wait()
     for copy in outs + slices + along_z + along_y + gathered + back:
         copy.wait_send()
-
-
-def ring(x, wide):
-    lon = x.shape[-1]
-    gap = jnp.zeros(x.shape[:-1] + (wide - lon - 2 * STEPS,), x.dtype)
-    return jnp.concatenate([x, x[..., :STEPS], gap, x[..., lon - STEPS :]], -1)
 
 
 def per_device(
@@ -343,21 +415,31 @@
     unit_wide = wide // halves
     y_ring = n_grid // z_ring
     count = own * n_mem
-    state = ring(background_elapsed_years.reshape(chunks, 8, levels, lon).transpose(0, 2, 1, 3), wide)
-    vk = ring(jnp.concatenate([currents[1, :, 0], diffusivity[:, 0]], 0), wide)
-    us = ring(currents[0, :, 0], wide)
-    sea = ring(sea_mask.astype(jnp.float32), wide)
     f32 = jnp.float32
     dma = pltpu.SemaphoreType.DMA
     halo_shape = (STEPS, chunks, levels, 8, wide)
+    i32 = jnp.int32
     scratch = [
-        pltpu.VMEM((STEPS - 1, chunks, levels, 8, wide), f32),
+        pltpu.VMEM((own, levels, 1, lon), f32),
+        pltpu.VMEM((2, levels, 1, lon), f32),
+        pltpu.VMEM((levels, 1, lon), f32),
+        pltpu.VMEM((1, lon), i32),
+        pltpu.VMEM((slots,), i32),
+        pltpu.VMEM((slots,), i32),
+        pltpu.SMEM((1,), i32),
+        pltpu.VMEM((slots,), f32),
+        pltpu.VMEM((slots,), f32),
         pltpu.VMEM(halo_shape, f32),
-        pltpu.VMEM(halo_shape, f32),
-        pltpu.VMEM((2 * levels, wide), f32),
-        pltpu.VMEM((2 * levels, wide), f32),
-        pltpu.VMEM((1, wide), f32),
-        pltpu.VMEM((1, wide), f32),
+        pltpu.VMEM((own, levels, 1, lon), f32),
+        pltpu.VMEM((own, levels, 1, lon), f32),
+        pltpu.VMEM((STEPS - 1,) + halo_shape[1:], f32),
+        pltpu.VMEM((STEPS - 1,) + halo_shape[1:], f32),
+        pltpu.VMEM((levels, 1, lon), f32),
+        pltpu.VMEM((levels, 1, lon), f32),
+        pltpu.VMEM((levels, 1, lon), f32),
+        pltpu.VMEM((levels, 1, lon), f32),
+        pltpu.VMEM((1, lon), i32),
+        pltpu.VMEM((1, lon), i32),
         pltpu.VMEM((levels, 7, 8, wide), f32),
         pltpu.VMEM((n_mem, chunks, 8, unit_wide), f32),
         pltpu.VMEM((count, unit_wide), f32),
@@ -365,39 +447,40 @@
         pltpu.VMEM((n_mem, own, count), f32),
         pltpu.VMEM((n_mem - 1, own, count), f32),
         pltpu.VMEM((own, count), f32),
+        pltpu.VMEM((y_ring - 1, own, count), f32),
+        pltpu.VMEM((own, count), f32),
         pltpu.VMEM((z_ring - 1, own, count), f32),
-        pltpu.VMEM((own, count), f32),
-        pltpu.VMEM((y_ring - 1, own, count), f32),
         pltpu.VMEM((own, count), f32),
         pltpu.VMEM((n_mem, own, count), f32),
         pltpu.VMEM((n_mem, own, unit_wide), f32),
+        pltpu.VMEM((levels, own, wide), f32),
+        pltpu.VMEM((levels, own, lon), f32),
     ]
     semaphores = [
+        dma((9,)),
         dma((2, STEPS, chunks)), dma((2, STEPS, chunks)),
-        dma((2, 2)), dma((2, 2)),
+        dma((2, 3)), dma((2, 3)),
         dma((n_mem - 1, chunks)), dma((n_mem - 1, chunks)),
         dma((n_mem - 1,)), dma((n_mem - 1,)),
         dma((z_ring - 1,)), dma((z_ring - 1,)),
         dma((y_ring - 1,)), dma((y_ring - 1,)),
         dma((n_mem - 1,)), dma((n_mem - 1,)),
         dma((n_mem - 1,)), dma((n_mem - 1,)),
+        dma((levels,)),
     ]
-    vmem = pl.BlockSpec(memory_space=pltpu.VMEM)
-    result = pl.pallas_call(
+    return pl.pallas_call(
         functools.partial(kernel, (n_grid, n_mem, z_ring, levels, wide, chunks)),
-        out_shape=jax.ShapeDtypeStruct((n_mem, own, unit_wide), f32),
-        in_specs=[vmem] * 9,
-        out_specs=vmem,
+        out_shape=jax.ShapeDtypeStruct((own, levels, 1, lon), f32),
+        in_specs=[pl.BlockSpec(memory_space=pltpu.HBM)] * 9,
+        out_specs=pl.BlockSpec(memory_space=pltpu.HBM),
         scratch_shapes=scratch + semaphores,
         compiler_params=pltpu.CompilerParams(
-            collective_id=0, has_side_effects=True, vmem_limit_bytes=40 * 1024 * 1024
+            collective_id=0, has_side_effects=True, vmem_limit_bytes=60 * 1024 * 1024
         ),
     )(
-        state, vk, us, sea, observed_cell[None], measured_layer_number[None], live_counts[None],
-        observed_value[None], error_variance[None],
+        background_elapsed_years, currents, diffusivity, sea_mask, observed_cell, measured_layer_number, live_counts,
+        observed_value, error_variance,
     )
-    whole = result.reshape(levels, halves, own, unit_wide).transpose(2, 0, 1, 3).reshape(own, levels, wide)
-    return whole[:, :, None, :lon]
 
 
 def solution(mesh):

time: 109 us -> 98.4 us (0.903)
  Pallas kernels: 102 us -> 95.8 us
  local copies, waits for them, and re-layouts: 6.15 us -> 1.78 us
    pallas_call x1, Pallas kernels: 102 us -> 95.8 us  [per_device(): pl.pallas_call(functools.partial(kernel, (n_grid, n_mem, z_ring, levels,...]
    transpose x2 -> x0, local copies, waits for them, and re-layouts: 1.42 us -> none  [the longest x1 1.12 us: per_device(): background_elapsed_years.reshape(chunks, 8, levels, lon)]
    unnamed x15 -> x1, local copies, waits for them, and re-layouts: 2.7 us -> 1.78 us
where the time goes in v2:
time: 98.4 us; the launch traced here: 98.3 us
  Pallas kernels  95.8 us (97%)
  local copies, waits for them, and re-layouts  1.78 us (2%)
    pallas_call x1, Pallas kernels, per_device(): pl.pallas_call(functools.partial(kernel, (n_grid, n_mem, z_ring, levels,...  95.8 us

profile of v2, /device:TPU:1, one launch (start us, length us, event | category | flops | bytes accessed | tf_op | source)
XLA Modules:
  0.0 98.3 jit_solution(5912830573443763493)
XLA Ops:
  0.7 95.8 %shard_map.91 = f32[16,4,1,1440]{3,2,1,0:T(1,128)} custom-call(f32[16,4,1,1440]{3,2,1,0:T(1,128)} %first_hbm.1, f32[2,4,1,1440]{3,2,1,0:T(1,128)} %currents_hbm.1, f32[4,1,1440]{2,1,0:T(1,128)} %kappa_hbm.1, s32[1,1440]{1,0:T(1,128)} %mask_hbm.1, s32[512]{0:T(512)} %cell_hbm.1, s32[512]{0:T(512)} %level_hbm.1, s32[1]{0:T(128)S(6)} %copy.11.live_hbm, ...), custom_call_target="tpu_custom_call" | custom-call | tf_op jit(solution)/shard_map/pallas_call | solution.py:471
  96.5 1.8 %copy.12 = f32[16,4,1,1440]{3,2,1,0:T(1,128)} copy(f32[16,4,1,1440]{3,2,1,0:T(1,128)} %shard_map.91) | data formatting | bytes 737280

commit v3 on v2

--- a/solution.py
+++ b/solution.py
@@ -80,6 +80,16 @@
     return jnp.concatenate(done, 0)
 
 
+def spread_row(flat, level, levels, lon, wide):
+    full, last = wide - LANES, lon - (wide - LANES)
+    body, packed = flat[:, level * full : (level + 1) * full], flat[:, levels * full :]
+    lane = lax.broadcasted_iota(jnp.int32, (8, LANES), 1)
+    ending = packed if level == 0 else pltpu.roll(packed, LANES - level * last, 1)
+    opening, closing = pltpu.roll(body[:, :LANES], last, 1), pltpu.roll(ending, LANES - last, 1)
+    tail = jnp.where(lane < last + STEPS, jnp.where(lane < last, ending, opening), 0.0)
+    return jnp.concatenate([body, jnp.where(lane >= LANES - STEPS, closing, tail)], 1)
+
+
 def ring(x, wide):
     rows, lon = x.shape
     gap = jnp.zeros((rows, wide - lon - 2 * STEPS), x.dtype)
@@ -91,12 +101,12 @@
     first_hbm, currents_hbm, kappa_hbm, mask_hbm, cell_hbm, level_hbm, live_hbm, value_hbm, variance_hbm,
     out_ref,
     first_ref, currents_ref, kappa_ref, mask_ref, cell_ref, level_ref, live_ref, value_ref, variance_ref,
-    states, raw_south, raw_north, from_south, from_north, v_south, v_north, k_south, k_north, mask_south, mask_north,
-    coefs, units, own_all, picks, part, slice_parts, y_own, y_parts, z_own, z_parts, total, gram, mixed, landed, final_ref,
+    states, leaving, raw_south, raw_north, from_south, from_north, v_south, v_north, k_south, k_north, mask_south, mask_north,
+    coefs, units, own_all, picks, part, slice_parts, y_own, y_parts, z_own, z_parts, total, gram, mixed, landed,
     s_in, s_halo, r_halo, s_static, r_static, s_out, r_out, s_slice, r_slice, s_z, r_z, s_y, r_y,
-    s_all, r_all, s_back, r_back, s_leave,
+    s_all, r_all, s_back, r_back,
 ):
-    n_grid, n_mem, z_ring, levels, wide, chunks = cfg
+    n_grid, n_mem, z_ring, levels, lon, wide, chunks = cfg
     y_ring = n_grid // z_ring
     own = 8 * chunks
     count = n_mem * own
@@ -165,7 +175,8 @@
             rows = pl.ds(8 * chunk, 8)
             src, below, above = first_hbm.at[rows], raw_south.at[rows], raw_north.at[rows]
         else:
-            src, below, above = states.at[step, chunk], from_south.at[step - 1, chunk], from_north.at[step - 1, chunk]
+            at = (step - 1, chunk)
+            src, below, above = leaving.at[at], from_south.at[at], from_north.at[at]
         up = remote(src, below, s_halo.at[0, step, chunk], r_halo.at[0, step, chunk], north)
         down = remote(src, above, s_halo.at[1, step, chunk], r_halo.at[1, step, chunk], south)
         return up, down
@@ -255,6 +266,9 @@
         for level in range(levels):
             coefs[level, index] = jnp.broadcast_to(values[level : level + 1], (8, wide))
 
+    full = wide - LANES
+    last_lanes = lon - full
+    tail_lane = lax.broadcasted_iota(jnp.int32, (8, LANES), 1)
     for step in range(STEPS):
         for chunk in range(chunks):
             up, down = halo(step, chunk)
@@ -267,7 +281,8 @@
                 if step == 0:
                     above, below = first_rows(raw_north, chunk, level), first_rows(raw_south, chunk, level)
                 else:
-                    above, below = from_north[step - 1, chunk, level], from_south[step - 1, chunk, level]
+                    above = spread_row(from_north.at[step - 1, chunk], level, levels, lon, wide)
+                    below = spread_row(from_south.at[step - 1, chunk], level, levels, lon, wide)
                 here = at(level)
                 around = at(level - 1) if level > 0 else 0.0
                 if level < levels - 1:
@@ -283,10 +298,14 @@
                 )
                 if step < STEPS - 1:
                     states[step + 1, chunk, level] = result
+                    leaving[step, chunk, :, level * full : (level + 1) * full] = result[:, :full]
+                    moved = result[:, full:] if level == 0 else pltpu.roll(result[:, full:], level * last_lanes, 1)
+                    packed = moved if level == 0 else jnp.where(tail_lane < level * last_lanes, packed, moved)
                 else:
                     for half in range(halves):
                         units[level * halves + half, chunk] = result[:, half * unit_wide : (half + 1) * unit_wide]
             if step < STEPS - 1:
+                leaving[step, chunk, :, levels * full :] = packed
                 start_halo(step + 1, chunk)
             else:
                 rows = pl.ds(pl.multiple_of(mem * own + 8 * chunk, 8), 8)
@@ -381,11 +400,8 @@
     landed[mine] = mixed[mem]
     for copy in back:
         copy.wait_recv()
-    leaving = []
     for level in range(levels):
-        final_ref[level] = landed[level][:, : final_ref.shape[2]]
-        leaving.append(pltpu.make_async_copy(final_ref.at[level], out_ref.at[:, level, 0, :], s_leave.at[level]))
-        leaving[-1].start()
+        out_ref[level] = landed[level][:, : out_ref.shape[2]]
 
     for step in range(STEPS):
         for chunk in range(chunks):
@@ -396,8 +412,6 @@
         pl.when(has_north)(copy.wait_send)
     for copy in static_down:
         pl.when(has_south)(copy.wait_send)
-    for copy in leaving:
-        copy.wait()
     for copy in outs + slices + along_z + along_y + gathered + back:
         copy.wait_send()
 
@@ -417,6 +431,7 @@
     count = own * n_mem
     f32 = jnp.float32
     dma = pltpu.SemaphoreType.DMA
+    packed_shape = (STEPS - 1, chunks, 8, levels * (wide - LANES) + LANES)
     halo_shape = (STEPS, chunks, levels, 8, wide)
     i32 = jnp.int32
     scratch = [
@@ -430,10 +445,11 @@
         pltpu.VMEM((slots,), f32),
         pltpu.VMEM((slots,), f32),
         pltpu.VMEM(halo_shape, f32),
+        pltpu.VMEM(packed_shape, f32),
         pltpu.VMEM((own, levels, 1, lon), f32),
         pltpu.VMEM((own, levels, 1, lon), f32),
-        pltpu.VMEM((STEPS - 1,) + halo_shape[1:], f32),
-        pltpu.VMEM((STEPS - 1,) + halo_shape[1:], f32),
+        pltpu.VMEM(packed_shape, f32),
+        pltpu.VMEM(packed_shape, f32),
         pltpu.VMEM((levels, 1, lon), f32),
         pltpu.VMEM((levels, 1, lon), f32),
         pltpu.VMEM((levels, 1, lon), f32),
@@ -454,7 +470,6 @@
         pltpu.VMEM((n_mem, own, count), f32),
         pltpu.VMEM((n_mem, own, unit_wide), f32),
         pltpu.VMEM((levels, own, wide), f32),
-        pltpu.VMEM((levels, own, lon), f32),
     ]
     semaphores = [
         dma((9,)),
@@ -466,13 +481,12 @@
         dma((y_ring - 1,)), dma((y_ring - 1,)),
         dma((n_mem - 1,)), dma((n_mem - 1,)),
         dma((n_mem - 1,)), dma((n_mem - 1,)),
-        dma((levels,)),
     ]
-    return pl.pallas_call(
-        functools.partial(kernel, (n_grid, n_mem, z_ring, levels, wide, chunks)),
-        out_shape=jax.ShapeDtypeStruct((own, levels, 1, lon), f32),
+    result = pl.pallas_call(
+        functools.partial(kernel, (n_grid, n_mem, z_ring, levels, lon, wide, chunks)),
+        out_shape=pltpu.VMEM((levels, own, lon), f32),
         in_specs=[pl.BlockSpec(memory_space=pltpu.HBM)] * 9,
-        out_specs=pl.BlockSpec(memory_space=pltpu.HBM),
+        out_specs=pl.BlockSpec(memory_space=pltpu.VMEM),
         scratch_shapes=scratch + semaphores,
         compiler_params=pltpu.CompilerParams(
             collective_id=0, has_side_effects=True, vmem_limit_bytes=60 * 1024 * 1024
@@ -481,6 +495,7 @@
         background_elapsed_years, currents, diffusivity, sea_mask, observed_cell, measured_layer_number, live_counts,
         observed_value, error_variance,
     )
+    return result.transpose(1, 0, 2)[:, :, None, :]
 
 
 def solution(mesh):

time: 98.4 us -> 95.5 us (0.971)
  Pallas kernels: 95.8 us -> 93.6 us
    pallas_call x1, Pallas kernels: 95.8 us -> 93.6 us  [per_device(): pl.pallas_call(functools.partial(kernel, (n_grid, n_mem, z_ring, levels,...]
    unnamed x1 -> x0, local copies, waits for them, and re-layouts: 1.78 us -> none
    broadcast_in_dim x0 -> x1, local copies, waits for them, and re-layouts: none -> 1.15 us  [per_device(): return result.transpose(1, 0, 2)[:, :, None, :]]
where the time goes in v3:
time: 95.5 us; the launch traced here: 95.4 us
  Pallas kernels  93.6 us (98%)
  local copies, waits for them, and re-layouts  1.15 us (1%)
    pallas_call x1, Pallas kernels, per_device(): pl.pallas_call(functools.partial(kernel, (n_grid, n_mem, z_ring, levels,...  93.6 us

profile of v3, /device:TPU:1, one launch (start us, length us, event | category | flops | bytes accessed | tf_op | source)
XLA Modules:
  0.0 95.4 jit_solution(16918307538712598940)
XLA Ops:
  0.7 93.6 %shard_map.91 = f32[4,16,1440]{2,1,0:T(8,128)S(1)} custom-call(f32[16,4,1,1440]{3,2,1,0:T(1,128)} %first_hbm.1, f32[2,4,1,1440]{3,2,1,0:T(1,128)} %currents_hbm.1, f32[4,1,1440]{2,1,0:T(1,128)} %kappa_hbm.1, s32[1,1440]{1,0:T(1,128)} %mask_hbm.1, s32[512]{0:T(512)} %cell_hbm.1, s32[512]{0:T(512)} %level_hbm.1, s32[1]{0:T(128)S(6)} %copy.11.live_hbm, ...), custom_call_target="tpu_custom_call" | custom-call | tf_op jit(solution)/shard_map/pallas_call | solution.py:485
  94.2 1.2 %copy.10 = f32[16,4,1,1440]{3,2,1,0:T(1,128)} copy(f32[16,4,1,1440]{3,0,1,2:T(8,128)S(1)} %bitcast.3) | data formatting | bytes 737280 | tf_op jit(solution)/shard_map/broadcast_in_dim | solution.py:498

commit v4 on v3

--- a/solution.py
+++ b/solution.py
@@ -80,9 +80,35 @@
     return jnp.concatenate(done, 0)
 
 
+def fold_square(square, count):
+    half = count // 2
+    row = lax.broadcasted_iota(jnp.int32, (half, count), 0)
+    lane = lax.broadcasted_iota(jnp.int32, (half, count), 1)
+    upper, lower = pltpu.roll(square[:half], half, 1), square[half:]
+    folded = jnp.where(jnp.logical_or(lane < half, row <= lane - half), upper, lower)
+    return folded, jnp.sum(jnp.where(row == lane - half, lower, 0.0), axis=0, keepdims=True)
+
+
+def unfold_square(folded, diagonal, count):
+    half = count // 2
+    row = lax.broadcasted_iota(jnp.int32, (count, count), 0)
+    lane = lax.broadcasted_iota(jnp.int32, (count, count), 1)
+    here = jnp.concatenate([pltpu.roll(folded, half, 1), folded], 0)
+    turned = jnp.transpose(here)
+    top = jnp.logical_and(row < half, row <= lane)
+    bottom = jnp.logical_and(lane >= half, row > lane)
+    square = jnp.where(jnp.logical_or(top, bottom), here, turned)
+    return jnp.where(jnp.logical_and(row == lane, row >= half), diagonal, square)
+
+
+def body_start(level, levels, full):
+    return level * full + (LANES if level >= levels // 2 else 0)
+
+
 def spread_row(flat, level, levels, lon, wide):
     full, last = wide - LANES, lon - (wide - LANES)
-    body, packed = flat[:, level * full : (level + 1) * full], flat[:, levels * full :]
+    start, shared = body_start(level, levels, full), levels // 2 * full
+    body, packed = flat[:, start : start + full], flat[:, shared : shared + LANES]
     lane = lax.broadcasted_iota(jnp.int32, (8, LANES), 1)
     ending = packed if level == 0 else pltpu.roll(packed, LANES - level * last, 1)
     opening, closing = pltpu.roll(body[:, :LANES], last, 1), pltpu.roll(ending, LANES - last, 1)
@@ -111,7 +137,9 @@
     own = 8 * chunks
     count = n_mem * own
     unit_wide = levels * wide // n_mem
-    halves = n_mem // levels
+    piece = unit_wide // 2
+    pieces, pair = wide // piece, levels // 2
+    full = wide - LANES
     grid = lax.axis_index("grid")
     mem = lax.axis_index("mem")
     y_at, z_at = grid // z_ring, lax.rem(grid, z_ring)
@@ -177,9 +205,22 @@
         else:
             at = (step - 1, chunk)
             src, below, above = leaving.at[at], from_south.at[at], from_north.at[at]
-        up = remote(src, below, s_halo.at[0, step, chunk], r_halo.at[0, step, chunk], north)
-        down = remote(src, above, s_halo.at[1, step, chunk], r_halo.at[1, step, chunk], south)
-        return up, down
+        if step < STEPS - 1:
+            trips = [(step, src, below, above)]
+        else:
+            early = pl.ds(0, pair * full + LANES)
+            late = pl.ds(pair * full + LANES, (levels - pair) * full)
+            trips = [
+                (step + index, src.at[:, lanes], below.at[:, lanes], above.at[:, lanes])
+                for index, lanes in enumerate((early, late))
+            ]
+        return [
+            (
+                remote(src, below, s_halo.at[0, at, chunk], r_halo.at[0, at, chunk], north),
+                remote(src, above, s_halo.at[1, at, chunk], r_halo.at[1, at, chunk], south),
+            )
+            for at, src, below, above in trips
+        ]
 
     statics = (currents_hbm.at[1], kappa_hbm, mask_hbm)
     static_up = [
@@ -192,9 +233,9 @@
     ]
 
     def start_halo(step, chunk):
-        up, down = halo(step, chunk)
-        pl.when(has_north)(up.start)
-        pl.when(has_south)(down.start)
+        for up, down in halo(step, chunk):
+            pl.when(has_north)(up.start)
+            pl.when(has_south)(down.start)
 
     for copy in static_up:
         pl.when(has_north)(copy.start)
@@ -228,8 +269,10 @@
         for level in range(levels):
             states[0, chunk, level] = first_rows(first_ref, chunk, level)
     slots = cell_ref.shape[0]
-    place = (level_ref[...] * wide + cell_ref[...]).reshape(1, slots) - mem * unit_wide
-    inside = jnp.logical_and(place >= 0, place < unit_wide)
+    upper_pair = jnp.where(level_ref[...] >= pair, 1, 0)
+    flat = (level_ref[...] - upper_pair * pair) * wide + cell_ref[...] - mem * piece
+    place = jnp.where(jnp.logical_and(flat >= 0, flat < piece), flat + upper_pair * piece, -1).reshape(1, slots)
+    inside = place >= 0
     live = lax.broadcasted_iota(jnp.int32, (1, slots), 1) < live_ref[0]
     weight = jnp.where(jnp.logical_and(inside, live), 1.0 / jnp.sqrt(variance_ref[...].reshape(1, slots)), 0.0)
     picks[...] = jnp.where(
@@ -266,15 +309,29 @@
         for level in range(levels):
             coefs[level, index] = jnp.broadcast_to(values[level : level + 1], (8, wide))
 
-    full = wide - LANES
+    def landing(chunk, which):
+        return pl.ds(pl.multiple_of(mem * own + 8 * chunk, 8), 8), pl.ds(which * piece, piece)
+
+    def sent(chunk, which):
+        return [
+            remote(
+                units.at[mem_peer(d), chunk, which], own_all.at[landing(chunk, which)],
+                s_out.at[d - 1, chunk, which], r_out.at[d - 1, chunk, which], {"mem": mem_peer(d)},
+            )
+            for d in range(1, n_mem)
+        ]
+
     last_lanes = lon - full
     tail_lane = lax.broadcasted_iota(jnp.int32, (8, LANES), 1)
     for step in range(STEPS):
         for chunk in range(chunks):
-            up, down = halo(step, chunk)
-            pl.when(has_south)(up.wait_recv)
-            pl.when(has_north)(down.wait_recv)
+            arriving = halo(step, chunk)
             for level in range(levels):
+                if level % (levels // len(arriving)) == 0:
+                    up, down = arriving[level * len(arriving) // levels]
+                    pl.when(has_south)(up.wait_recv)
+                    pl.when(has_north)(down.wait_recv)
+
                 def at(which):
                     return states[step, chunk, which]
 
@@ -298,36 +355,28 @@
                 )
                 if step < STEPS - 1:
                     states[step + 1, chunk, level] = result
-                    leaving[step, chunk, :, level * full : (level + 1) * full] = result[:, :full]
+                    start = body_start(level, levels, full)
+                    leaving[step, chunk, :, start : start + full] = result[:, :full]
                     moved = result[:, full:] if level == 0 else pltpu.roll(result[:, full:], level * last_lanes, 1)
                     packed = moved if level == 0 else jnp.where(tail_lane < level * last_lanes, packed, moved)
                 else:
-                    for half in range(halves):
-                        units[level * halves + half, chunk] = result[:, half * unit_wide : (half + 1) * unit_wide]
+                    for index in range(pieces):
+                        units[level % pair * pieces + index, chunk, level // pair] = result[
+                            :, index * piece : (index + 1) * piece
+                        ]
+                    if level % pair == pair - 1:
+                        for copy in sent(chunk, level // pair):
+                            copy.start()
+                        rows, lanes = landing(chunk, level // pair)
+                        own_all[rows, lanes] = units[mem, chunk, level // pair]
             if step < STEPS - 1:
-                leaving[step, chunk, :, levels * full :] = packed
+                leaving[step, chunk, :, pair * full : pair * full + LANES] = packed
                 start_halo(step + 1, chunk)
-            else:
-                rows = pl.ds(pl.multiple_of(mem * own + 8 * chunk, 8), 8)
-                for d in range(1, n_mem):
-                    remote(
-                        units.at[mem_peer(d), chunk], own_all.at[rows], s_out.at[d - 1, chunk], r_out.at[d - 1, chunk],
-                        {"mem": mem_peer(d)},
-                    ).start()
-                own_all[rows, :] = units[mem, chunk]
 
     def exchange(src_of, dst_of, send, recv, peers, axis, peer):
         return [remote(src_of(d), dst_of(d), send.at[d - 1], recv.at[d - 1], {axis: peer(d)}) for d in range(1, peers)]
 
-    outs = [
-        remote(
-            units.at[mem_peer(d), chunk],
-            own_all.at[pl.ds(pl.multiple_of(mem * own + 8 * chunk, 8), 8)],
-            s_out.at[d - 1, chunk], r_out.at[d - 1, chunk], {"mem": mem_peer(d)},
-        )
-        for d in range(1, n_mem)
-        for chunk in range(chunks)
-    ]
+    outs = [copy for chunk in range(chunks) for which in range(2) for copy in sent(chunk, which)]
     for copy in outs:
         copy.wait_recv()
 
@@ -348,9 +397,13 @@
     final = seen[count - 1 : count]
     shared = -inner * (everyone - final) - final / root
     stacked = jnp.where(last, value_ref[...].reshape(1, slots) - everyone / count, seen + shared) * weight
-    part[...] = lax.dot_general(
+    folded, diagonal = fold_square(lax.dot_general(
         stacked, stacked, (((1,), (1,)), ((), ())), precision=HIGHEST, preferred_element_type=jnp.float32
-    ).reshape(n_mem, own, count)
+    ), count)
+    share = count // 2 // n_mem
+    for index in range(n_mem):
+        part[index, :share] = folded[index * share : (index + 1) * share]
+        part[index, share:] = diagonal
 
     slices = exchange(lambda d: part.at[mem_peer(d)], lambda d: slice_parts.at[d - 1], s_slice, r_slice, n_mem, "mem", mem_peer)
     for copy in slices:
@@ -377,7 +430,8 @@
     for copy in gathered:
         copy.wait_recv()
 
-    inverse = factor_inverse(gram[...].reshape(count, count), count)
+    folded = jnp.concatenate([gram[index, :share] for index in range(n_mem)], 0)
+    inverse = factor_inverse(unfold_square(folded, gram[0, share:], count), count)
     square_lane = lax.broadcasted_iota(jnp.int32, (count, count), 1)
     square_row = lax.broadcasted_iota(jnp.int32, (count, count), 0)
     leading = jnp.where(square_lane < count - 1, inverse, 0.0)
@@ -389,25 +443,25 @@
     spread = jnp.where(square_row == count - 1, -down_sum / root, kept - inner * down_sum)
     mixing = 1.0 / count + shift + math.sqrt(count - 1) * spread
     mixed[...] = jnp.dot(mixing, own_all[...], precision=HIGHEST).reshape(n_mem, own, unit_wide)
-    mine = (
-        mem // halves,
-        slice(None),
-        pl.ds(pl.multiple_of(lax.rem(mem, halves) * unit_wide, LANES), unit_wide),
-    )
-    back = exchange(lambda d: mixed.at[mem_peer(d)], lambda d: landed.at[mine], s_back, r_back, n_mem, "mem", mem_peer)
+    back = exchange(lambda d: mixed.at[mem_peer(d)], lambda d: landed.at[mem], s_back, r_back, n_mem, "mem", mem_peer)
     for copy in back:
         copy.start()
-    landed[mine] = mixed[mem]
+    landed[mem] = mixed[mem]
     for copy in back:
         copy.wait_recv()
-    for level in range(levels):
-        out_ref[level] = landed[level][:, : out_ref.shape[2]]
+    for member in range(n_mem):
+        for which in range(2):
+            lane = member % pieces * piece
+            count_here = min(piece, lon - lane)
+            out_ref[which * pair + member // pieces, :, lane : lane + count_here] = landed[
+                member, :, which * piece : which * piece + count_here
+            ]
 
     for step in range(STEPS):
         for chunk in range(chunks):
-            up, down = halo(step, chunk)
-            pl.when(has_north)(up.wait_send)
-            pl.when(has_south)(down.wait_send)
+            for up, down in halo(step, chunk):
+                pl.when(has_north)(up.wait_send)
+                pl.when(has_south)(down.wait_send)
     for copy in static_up:
         pl.when(has_north)(copy.wait_send)
     for copy in static_down:
@@ -426,7 +480,7 @@
     halves = n_mem // levels
     block = LANES * halves
     wide = -(-(lon + 2 * STEPS) // block) * block
-    unit_wide = wide // halves
+    unit_wide = levels * wide // n_mem
     y_ring = n_grid // z_ring
     count = own * n_mem
     f32 = jnp.float32
@@ -457,25 +511,25 @@
         pltpu.VMEM((1, lon), i32),
         pltpu.VMEM((1, lon), i32),
         pltpu.VMEM((levels, 7, 8, wide), f32),
-        pltpu.VMEM((n_mem, chunks, 8, unit_wide), f32),
+        pltpu.VMEM((n_mem, chunks, 2, 8, unit_wide // 2), f32),
         pltpu.VMEM((count, unit_wide), f32),
         pltpu.VMEM((unit_wide, slots), jnp.bfloat16),
-        pltpu.VMEM((n_mem, own, count), f32),
-        pltpu.VMEM((n_mem - 1, own, count), f32),
-        pltpu.VMEM((own, count), f32),
-        pltpu.VMEM((y_ring - 1, own, count), f32),
-        pltpu.VMEM((own, count), f32),
-        pltpu.VMEM((z_ring - 1, own, count), f32),
-        pltpu.VMEM((own, count), f32),
-        pltpu.VMEM((n_mem, own, count), f32),
+        pltpu.VMEM((n_mem, count // 2 // n_mem + 1, count), f32),
+        pltpu.VMEM((n_mem - 1, count // 2 // n_mem + 1, count), f32),
+        pltpu.VMEM((count // 2 // n_mem + 1, count), f32),
+        pltpu.VMEM((y_ring - 1, count // 2 // n_mem + 1, count), f32),
+        pltpu.VMEM((count // 2 // n_mem + 1, count), f32),
+        pltpu.VMEM((z_ring - 1, count // 2 // n_mem + 1, count), f32),
+        pltpu.VMEM((count // 2 // n_mem + 1, count), f32),
+        pltpu.VMEM((n_mem, count // 2 // n_mem + 1, count), f32),
         pltpu.VMEM((n_mem, own, unit_wide), f32),
-        pltpu.VMEM((levels, own, wide), f32),
+        pltpu.VMEM((n_mem, own, unit_wide), f32),
     ]
     semaphores = [
         dma((9,)),
-        dma((2, STEPS, chunks)), dma((2, STEPS, chunks)),
+        dma((2, STEPS + 1, chunks)), dma((2, STEPS + 1, chunks)),
         dma((2, 3)), dma((2, 3)),
-        dma((n_mem - 1, chunks)), dma((n_mem - 1, chunks)),
+        dma((n_mem - 1, chunks, 2)), dma((n_mem - 1, chunks, 2)),
         dma((n_mem - 1,)), dma((n_mem - 1,)),
         dma((z_ring - 1,)), dma((z_ring - 1,)),
         dma((y_ring - 1,)), dma((y_ring - 1,)),

time: 95.5 us -> 93.9 us (0.983)
  Pallas kernels: 93.6 us -> 92 us
    pallas_call x1, Pallas kernels: 93.6 us -> 92 us  [per_device(): pl.pallas_call(functools.partial(kernel, (n_grid, n_mem, z_ring, levels,...]
where the time goes in v4:
time: 93.9 us; the launch traced here: 93.8 us
  Pallas kernels  92 us (98%)
  local copies, waits for them, and re-layouts  1.15 us (1%)
    pallas_call x1, Pallas kernels, per_device(): pl.pallas_call(functools.partial(kernel, (n_grid, n_mem, z_ring, levels,...  92 us

profile of v4, /device:TPU:1, one launch (start us, length us, event | category | flops | bytes accessed | tf_op | source)
XLA Modules:
  0.0 93.8 jit_solution(8905649571447120564)
XLA Ops:
  0.7 92.0 %shard_map.91 = f32[4,16,1440]{2,1,0:T(8,128)S(1)} custom-call(f32[16,4,1,1440]{3,2,1,0:T(1,128)} %first_hbm.1, f32[2,4,1,1440]{3,2,1,0:T(1,128)} %currents_hbm.1, f32[4,1,1440]{2,1,0:T(1,128)} %kappa_hbm.1, s32[1,1440]{1,0:T(1,128)} %mask_hbm.1, s32[512]{0:T(512)} %cell_hbm.1, s32[512]{0:T(512)} %level_hbm.1, s32[1]{0:T(128)S(6)} %copy.11.live_hbm, ...), custom_call_target="tpu_custom_call" | custom-call | tf_op jit(solution)/shard_map/pallas_call | solution.py:539
  92.6 1.2 %copy.10 = f32[16,4,1,1440]{3,2,1,0:T(1,128)} copy(f32[16,4,1,1440]{3,0,1,2:T(8,128)S(1)} %bitcast.3) | data formatting | bytes 737280 | tf_op jit(solution)/shard_map/broadcast_in_dim | solution.py:552

commit v5 on v4

--- a/solution.py
+++ b/solution.py
@@ -101,6 +101,10 @@
     return jnp.where(jnp.logical_and(row == lane, row >= half), diagonal, square)
 
 
+def far_first(peers):
+    return sorted(range(1, peers), key=lambda d: -min(d, peers - d))
+
+
 def body_start(level, levels, full):
     return level * full + (LANES if level >= levels // 2 else 0)
 
@@ -182,11 +186,11 @@
     def _():
         greet({"grid": grid - 1})
 
-    for d in sorted(range(1, z_ring), key=lambda d: min(d, z_ring - d)):
+    for d in far_first(z_ring):
         greet({"grid": z_peer(d)})
-    for d in range(1, y_ring):
+    for d in far_first(y_ring):
         greet({"grid": y_peer(d)})
-    for d in range(1, n_mem):
+    for d in far_first(n_mem):
         greet({"mem": mem_peer(d)})
     greeted = z_ring + y_ring + n_mem - 3 + cross_north.astype(jnp.int32) + cross_south.astype(jnp.int32)
     pl.semaphore_wait(barrier, greeted)
@@ -318,7 +322,7 @@
                 units.at[mem_peer(d), chunk, which], own_all.at[landing(chunk, which)],
                 s_out.at[d - 1, chunk, which], r_out.at[d - 1, chunk, which], {"mem": mem_peer(d)},
             )
-            for d in range(1, n_mem)
+            for d in far_first(n_mem)
         ]
 
     last_lanes = lon - full
@@ -374,7 +378,7 @@
                 start_halo(step + 1, chunk)
 
     def exchange(src_of, dst_of, send, recv, peers, axis, peer):
-        return [remote(src_of(d), dst_of(d), send.at[d - 1], recv.at[d - 1], {axis: peer(d)}) for d in range(1, peers)]
+        return [remote(src_of(d), dst_of(d), send.at[d - 1], recv.at[d - 1], {axis: peer(d)}) for d in far_first(peers)]
 
     outs = [copy for chunk in range(chunks) for which in range(2) for copy in sent(chunk, which)]
     for copy in outs:

time: 93.9 us -> 92.4 us (0.984)
  Pallas kernels: 92 us -> 90.4 us
    pallas_call x1, Pallas kernels: 92 us -> 90.4 us  [per_device(): pl.pallas_call(functools.partial(kernel, (n_grid, n_mem, z_ring, levels,...]
where the time goes in v5:
time: 92.4 us; the launch traced here: 92.2 us
  Pallas kernels  90.4 us (98%)
  local copies, waits for them, and re-layouts  1.15 us (1%)
    pallas_call x1, Pallas kernels, per_device(): pl.pallas_call(functools.partial(kernel, (n_grid, n_mem, z_ring, levels,...  90.4 us

profile of v5, /device:TPU:1, one launch (start us, length us, event | category | flops | bytes accessed | tf_op | source)
XLA Modules:
  0.0 92.2 jit_solution(10645545500115321984)
XLA Ops:
  0.7 90.4 %shard_map.91 = f32[4,16,1440]{2,1,0:T(8,128)S(1)} custom-call(f32[16,4,1,1440]{3,2,1,0:T(1,128)} %first_hbm.1, f32[2,4,1,1440]{3,2,1,0:T(1,128)} %currents_hbm.1, f32[4,1,1440]{2,1,0:T(1,128)} %kappa_hbm.1, s32[1,1440]{1,0:T(1,128)} %mask_hbm.1, s32[512]{0:T(512)} %cell_hbm.1, s32[512]{0:T(512)} %level_hbm.1, s32[1]{0:T(128)S(6)} %copy.11.live_hbm, ...), custom_call_target="tpu_custom_call" | custom-call | tf_op jit(solution)/shard_map/pallas_call | solution.py:543
  91.1 1.2 %copy.10 = f32[16,4,1,1440]{3,2,1,0:T(1,128)} copy(f32[16,4,1,1440]{3,0,1,2:T(8,128)S(1)} %bitcast.3) | data formatting | bytes 737280 | tf_op jit(solution)/shard_map/broadcast_in_dim | solution.py:556

commit v6 on v3

--- a/solution.py
+++ b/solution.py
@@ -80,6 +80,31 @@
     return jnp.concatenate(done, 0)
 
 
+def fold_square(square, count):
+    half = count // 2
+    row = lax.broadcasted_iota(jnp.int32, (half, count), 0)
+    lane = lax.broadcasted_iota(jnp.int32, (half, count), 1)
+    upper, lower = pltpu.roll(square[:half], half, 1), square[half:]
+    folded = jnp.where(jnp.logical_or(lane < half, row <= lane - half), upper, lower)
+    return folded, jnp.sum(jnp.where(row == lane - half, lower, 0.0), axis=0, keepdims=True)
+
+
+def unfold_square(folded, diagonal, count):
+    half = count // 2
+    row = lax.broadcasted_iota(jnp.int32, (count, count), 0)
+    lane = lax.broadcasted_iota(jnp.int32, (count, count), 1)
+    here = jnp.concatenate([pltpu.roll(folded, half, 1), folded], 0)
+    turned = jnp.transpose(here)
+    top = jnp.logical_and(row < half, row <= lane)
+    bottom = jnp.logical_and(lane >= half, row > lane)
+    square = jnp.where(jnp.logical_or(top, bottom), here, turned)
+    return jnp.where(jnp.logical_and(row == lane, row >= half), diagonal, square)
+
+
+def far_first(peers):
+    return sorted(range(1, peers), key=lambda d: -min(d, peers - d))
+
+
 def spread_row(flat, level, levels, lon, wide):
     full, last = wide - LANES, lon - (wide - LANES)
     body, packed = flat[:, level * full : (level + 1) * full], flat[:, levels * full :]
@@ -154,11 +179,11 @@
     def _():
         greet({"grid": grid - 1})
 
-    for d in sorted(range(1, z_ring), key=lambda d: min(d, z_ring - d)):
+    for d in far_first(z_ring):
         greet({"grid": z_peer(d)})
-    for d in range(1, y_ring):
+    for d in far_first(y_ring):
         greet({"grid": y_peer(d)})
-    for d in range(1, n_mem):
+    for d in far_first(n_mem):
         greet({"mem": mem_peer(d)})
     greeted = z_ring + y_ring + n_mem - 3 + cross_north.astype(jnp.int32) + cross_south.astype(jnp.int32)
     pl.semaphore_wait(barrier, greeted)
@@ -309,7 +334,7 @@
                 start_halo(step + 1, chunk)
             else:
                 rows = pl.ds(pl.multiple_of(mem * own + 8 * chunk, 8), 8)
-                for d in range(1, n_mem):
+                for d in far_first(n_mem):
                     remote(
                         units.at[mem_peer(d), chunk], own_all.at[rows], s_out.at[d - 1, chunk], r_out.at[d - 1, chunk],
                         {"mem": mem_peer(d)},
@@ -317,7 +342,7 @@
                 own_all[rows, :] = units[mem, chunk]
 
     def exchange(src_of, dst_of, send, recv, peers, axis, peer):
-        return [remote(src_of(d), dst_of(d), send.at[d - 1], recv.at[d - 1], {axis: peer(d)}) for d in range(1, peers)]
+        return [remote(src_of(d), dst_of(d), send.at[d - 1], recv.at[d - 1], {axis: peer(d)}) for d in far_first(peers)]
 
     outs = [
         remote(
@@ -348,9 +373,13 @@
     final = seen[count - 1 : count]
     shared = -inner * (everyone - final) - final / root
     stacked = jnp.where(last, value_ref[...].reshape(1, slots) - everyone / count, seen + shared) * weight
-    part[...] = lax.dot_general(
+    folded, diagonal = fold_square(lax.dot_general(
         stacked, stacked, (((1,), (1,)), ((), ())), precision=HIGHEST, preferred_element_type=jnp.float32
-    ).reshape(n_mem, own, count)
+    ), count)
+    share = count // 2 // n_mem
+    for index in range(n_mem):
+        part[index, :share] = folded[index * share : (index + 1) * share]
+        part[index, share:] = diagonal
 
     slices = exchange(lambda d: part.at[mem_peer(d)], lambda d: slice_parts.at[d - 1], s_slice, r_slice, n_mem, "mem", mem_peer)
     for copy in slices:
@@ -377,7 +406,8 @@
     for copy in gathered:
         copy.wait_recv()
 
-    inverse = factor_inverse(gram[...].reshape(count, count), count)
+    folded = jnp.concatenate([gram[index, :share] for index in range(n_mem)], 0)
+    inverse = factor_inverse(unfold_square(folded, gram[0, share:], count), count)
     square_lane = lax.broadcasted_iota(jnp.int32, (count, count), 1)
     square_row = lax.broadcasted_iota(jnp.int32, (count, count), 0)
     leading = jnp.where(square_lane < count - 1, inverse, 0.0)
@@ -460,14 +490,14 @@
         pltpu.VMEM((n_mem, chunks, 8, unit_wide), f32),
         pltpu.VMEM((count, unit_wide), f32),
         pltpu.VMEM((unit_wide, slots), jnp.bfloat16),
-        pltpu.VMEM((n_mem, own, count), f32),
-        pltpu.VMEM((n_mem - 1, own, count), f32),
-        pltpu.VMEM((own, count), f32),
-        pltpu.VMEM((y_ring - 1, own, count), f32),
-        pltpu.VMEM((own, count), f32),
-        pltpu.VMEM((z_ring - 1, own, count), f32),
-        pltpu.VMEM((own, count), f32),
-        pltpu.VMEM((n_mem, own, count), f32),
+        pltpu.VMEM((n_mem, count // 2 // n_mem + 1, count), f32),
+        pltpu.VMEM((n_mem - 1, count // 2 // n_mem + 1, count), f32),
+        pltpu.VMEM((count // 2 // n_mem + 1, count), f32),
+        pltpu.VMEM((y_ring - 1, count // 2 // n_mem + 1, count), f32),
+        pltpu.VMEM((count // 2 // n_mem + 1, count), f32),
+        pltpu.VMEM((z_ring - 1, count // 2 // n_mem + 1, count), f32),
+        pltpu.VMEM((count // 2 // n_mem + 1, count), f32),
+        pltpu.VMEM((n_mem, count // 2 // n_mem + 1, count), f32),
         pltpu.VMEM((n_mem, own, unit_wide), f32),
         pltpu.VMEM((levels, own, wide), f32),
     ]

time: 95.5 us -> 92.4 us (0.968)
  Pallas kernels: 93.6 us -> 90.5 us
    pallas_call x1, Pallas kernels: 93.6 us -> 90.5 us  [per_device(): pl.pallas_call(functools.partial(kernel, (n_grid, n_mem, z_ring, levels,...]
where the time goes in v6:
time: 92.4 us; the launch traced here: 92.3 us
  Pallas kernels  90.5 us (98%)
  local copies, waits for them, and re-layouts  1.15 us (1%)
    pallas_call x1, Pallas kernels, per_device(): pl.pallas_call(functools.partial(kernel, (n_grid, n_mem, z_ring, levels,...  90.5 us

profile of v6, /device:TPU:1, one launch (start us, length us, event | category | flops | bytes accessed | tf_op | source)
XLA Modules:
  0.0 92.3 jit_solution(8569696695917773033)
XLA Ops:
  0.7 90.5 %shard_map.91 = f32[4,16,1440]{2,1,0:T(8,128)S(1)} custom-call(f32[16,4,1,1440]{3,2,1,0:T(1,128)} %first_hbm.1, f32[2,4,1,1440]{3,2,1,0:T(1,128)} %currents_hbm.1, f32[4,1,1440]{2,1,0:T(1,128)} %kappa_hbm.1, s32[1,1440]{1,0:T(1,128)} %mask_hbm.1, s32[512]{0:T(512)} %cell_hbm.1, s32[512]{0:T(512)} %level_hbm.1, s32[1]{0:T(128)S(6)} %copy.11.live_hbm, ...), custom_call_target="tpu_custom_call" | custom-call | tf_op jit(solution)/shard_map/pallas_call | solution.py:515
  91.1 1.2 %copy.10 = f32[16,4,1,1440]{3,2,1,0:T(1,128)} copy(f32[16,4,1,1440]{3,0,1,2:T(8,128)S(1)} %bitcast.3) | data formatting | bytes 737280 | tf_op jit(solution)/shard_map/broadcast_in_dim | solution.py:528
